TPU v7x, 32 devices: a whole 2x2x4 slice. The times are simulated.
32 devices in a mesh: dp: 8 (over z, x), row: 2 (over core), col: 2 (over y).
Axes of the slice: x: 2, y: 2, z: 4, core: 2. Of those that a mesh axis runs over, the one named last changes fastest.
Arguments:
- tokens_in: bfloat16 [16384, 768], P(('dp', 'row'), 'col'), may hold values from -6 to 6
- teacher: bfloat16 [16384, 768], P(('dp', 'row'), 'col'), may hold values from -6 to 6
- qkv_weight: bfloat16 [2, 768, 3, 768], P(None, 'col', None, 'row'), may hold values from -0.21875 to 0.21875
- query_bias: float32 [2, 768], P(None, 'row'), may hold values from -3 to 3
- out_weight: bfloat16 [2, 768, 768], P(None, 'row', 'col'), may hold values from -2.5 to 2.5
- out_bias: float32 [2, 768], P(None, 'col'), may hold values from -3 to 3
- first_gain: float32 [2, 768], P(None, 'col'), may hold values from 0.25 to 1.75
- first_shift: float32 [2, 768], P(None, 'col'), may hold values from -3 to 3
- up_weight: bfloat16 [2, 768, 3072], P(None, 'col', 'row'), may hold values from -0.21875 to 0.21875
- up_bias: float32 [2, 3072], P(None, 'row'), may hold values from -3 to 3
- down_weight: bfloat16 [2, 3072, 768], P(None, 'row', 'col'), may hold values from -0.109375 to 0.109375
- down_bias: float32 [2, 768], P(None, 'col'), may hold values from -3 to 3
- second_gain: float32 [2, 768], P(None, 'col'), may hold values from 0.25 to 1.75
- second_shift: float32 [2, 768], P(None, 'col'), may hold values from -3 to 3
- random_blocks: int32 [2, 12, 14, 3], replicated, may hold values from 0 to 15
- segment_ids: int32 [16, 1024], P('dp'), may hold values from 0 to 3, never falling along the last dimension, each value on 1 to 512 neighbouring positions
- padding_mask: int32 [16, 1024], P('dp'), may hold values from 0 to 1, as said below
Outputs:
- hidden_out: float32 [16384, 768], P(('dp', 'row'), 'col')
- loss: float32 [], replicated
- input_grad: float32 [16384, 768], P(('dp', 'row'), 'col')
- grad_query_key_weight: float32 [2, 768, 2, 768], P(None, 'col', None, 'row')
- grad_value_weight: float32 [2, 768, 768], P(None, 'col', 'row')
- grad_query_bias: float32 [2, 768], P(None, 'row')
- grad_out_weight: float32 [2, 768, 768], P(None, 'row', 'col')
- grad_out_bias: float32 [2, 768], P(None, 'col')
- grad_first_gain: float32 [2, 768], P(None, 'col')
- grad_first_shift: float32 [2, 768], P(None, 'col')
- grad_up_weight: float32 [2, 768, 3072], P(None, 'col', 'row')
- grad_up_bias: float32 [2, 3072], P(None, 'row')
- grad_down_weight: float32 [2, 3072, 768], P(None, 'row', 'col')
- grad_down_bias: float32 [2, 768], P(None, 'col')
- grad_second_gain: float32 [2, 768], P(None, 'col')
- grad_second_shift: float32 [2, 768], P(None, 'col')
Inputs may be any that keep to these rules, and one draw needn't show every extreme that they name: `padding_mask`: 1 marks a real token; the real tokens of each sequence form its prefix, one token long at least.
All inputs are finite; a program needn't handle non-finite values.
Results may differ from a plain program's by a relative error of at most 0.03.
Values may be sent and summed in bfloat16 or wider, within the bound.
No kernel may reach another device: no remote copies, remote signals or barrier semaphores. Data moves between devices by JAX's collectives and lax.ppermute only.
A program may use at most 256 MiB of HBM per device.

v0:
```python
from functools import partial
from types import SimpleNamespace

import jax
import jax.numpy as jnp
from jax import lax
from jax.experimental import pallas as pl
from jax.experimental.pallas import tpu as pltpu
from jax.sharding import PartitionSpec as P

BLK = 64
EPSILON = 1e-06
MASKED_SCORE = -1e30
LANES = 128
SMALL_SLOTS = 8
TOKEN_BLOCK = 512
LAYERS = 2
QKV, OUT, UP, DOWN = range(4)
WHOLE, ROWS, SUM = -1, -2, -3
SCATTER, ADD, GATHER = range(3)
DP, ROW, COL = "dp", "row", "col"
VMEM_LIMIT = 48 * 1024 * 1024
GELU_SCALE = (2.0 / 3.141592653589793) ** 0.5
GELU_CUBE = 0.044715
BF16 = jnp.bfloat16
F32 = jnp.float32


def after(value, *before):
    return lax.optimization_barrier((value,) + before)[0]


def swap(value, axis):
    return lax.ppermute(value, axis, [(0, 1), (1, 0)])


def swap_bit(value, bit):
    count = lax.axis_size(DP)
    return lax.ppermute(value, DP, [(i, i ^ (1 << bit)) for i in range(count)])


def dp_bits():
    return (lax.axis_size(DP) - 1).bit_length()


def own_half(value, bit):
    halves = value.reshape(2, value.shape[0] // 2, value.shape[1])
    place = (lax.axis_index(DP) >> bit) & 1
    mine = lax.dynamic_index_in_dim(halves, place, 0, keepdims=False)
    other = lax.dynamic_index_in_dim(halves, 1 - place, 0, keepdims=False)
    return mine, other


def join_halves(mine, other, bit):
    place = (lax.axis_index(DP) >> bit) & 1
    return jnp.where(
        place == 0,
        jnp.concatenate([mine, other], axis=0),
        jnp.concatenate([other, mine], axis=0),
    )


class Line:
    def __init__(self):
        self.last = ()

    def next(self, value):
        return after(value, *self.last) if self.last else value

    def mark(self, *values):
        self.last = values
        return values[0]


class Fetch:
    def __init__(self, line, stack, layer, bit):
        self.bit = None if bit is None else min(bit, dp_bits() - 1)
        rows = stack.shape[1]
        if bit is None:
            piece = line.next(stack)[layer]
        else:
            start = (layer, ((lax.axis_index(DP) >> self.bit) & 1) * (rows // 2)) + (0,) * (stack.ndim - 2)
            rows = rows // 2
            piece = lax.dynamic_slice(line.next(stack), start, (1, rows) + stack.shape[2:])
        self.pieces = [swap(line.mark(piece.reshape(rows, -1)), COL)]

    def pass_on(self, line):
        self.pieces[0] = line.mark(line.next(self.pieces[0]))
        self.pieces.append(swap_bit(self.pieces[0], self.bit))

    def arrived(self, line):
        self.pieces[-1] = line.mark(line.next(self.pieces[-1]))


class Reduce:
    def __init__(self, other, wide):
        self.got, self.joins, self.parts = swap(other, COL), None, None
        bits = dp_bits()
        if wide and bits > 2:
            middle = [(SCATTER, 1)] + [(ADD, bit) for bit in range(2, bits)] + [(GATHER, 1)]
        else:
            middle = [(ADD, bit) for bit in range(1, bits)]
        self.plan = [(SCATTER, 0)] + middle + [(GATHER, 0)]

    def done(self):
        return self.plan is None

    def step(self, line):
        if self.done():
            return
        got = line.next(self.got)
        if not self.plan:
            self.plan, self.got = None, line.mark(got)
            return
        if self.joins is not None:
            parts = [join_halves(self.sent, got, self.joins)]
        else:
            parts = (self.parts or [self.own]) + [got]
        (kind, bit), self.plan = self.plan[0], self.plan[1:]
        self.joins = None
        if kind == SCATTER:
            halves = [own_half(part, bit) for part in parts]
            self.parts = [mine for mine, _ in halves]
            parts = [other for _, other in halves]
        self.sent = sum(part.astype(F32) for part in parts).astype(BF16)
        if kind == ADD:
            self.parts = [self.sent]
        elif kind == GATHER:
            self.joins = bit
        self.got = swap_bit(line.mark(self.sent), bit)

    def halves(self):
        return self.sent, self.got


def attention_tables(segment, valid, random_blocks, pair_heads):
    layers, heads, middle, extra = random_blocks.shape
    length = segment.shape[0]
    blocks = length // BLK
    position = jnp.arange(length, dtype=jnp.int32)
    codes = jnp.where(valid > 0, segment, length + position)
    index = jnp.arange(1, blocks - 1, dtype=jnp.int32)
    window = jnp.stack(
        [jnp.zeros_like(index), jnp.full_like(index, blocks - 1), index - 1, index, index + 1],
        axis=1,
    )
    window = jnp.broadcast_to(window, random_blocks.shape[:-1] + (5,))
    listed = jnp.concatenate([window, random_blocks], axis=-1)
    total = listed.shape[-1]
    earlier = jnp.arange(total)[:, None] > jnp.arange(total)[None, :]
    kept = ~jnp.any((listed[..., :, None] == listed[..., None, :]) & earlier, axis=-1)
    real = (valid > 0).reshape(blocks, BLK)
    ids = segment.reshape(blocks, BLK)
    big = jnp.int32(1 << 20)
    low = jnp.min(jnp.where(real, ids, big), axis=1)
    high = jnp.max(jnp.where(real, ids, -big), axis=1)
    live = (low[:, None] <= high[None, :]) & (low[None, :] <= high[:, None])
    live = live | (jnp.arange(blocks)[:, None] == jnp.arange(blocks)[None, :])
    chosen = listed[..., None] == jnp.arange(blocks, dtype=jnp.int32)
    kept = kept & jnp.any(chosen & live[1 : blocks - 1][:, None, :], axis=-1)
    pairs = heads // pair_heads
    listed = listed.reshape(layers, pairs, pair_heads, middle, total)
    kept = kept.reshape(layers, pairs, pair_heads, middle, total)
    shared = [listed[:, :, 0, :, :5]] + [listed[:, :, h, :, 5:] for h in range(pair_heads)]
    used = [kept[:, :, 0, :, :5]] + [kept[:, :, h, :, 5:] for h in range(pair_heads)]
    shared, used = jnp.concatenate(shared, axis=-1), jnp.concatenate(used, axis=-1)
    slots = 5 + extra * pair_heads
    which = [0] * 5
    for h in range(pair_heads):
        which += [h + 1] * extra
    which = jnp.broadcast_to(jnp.array(which, jnp.int32), shared.shape)
    entry = shared | (jnp.where(used, shared, blocks) << 8) | (which << 16)
    sums = jnp.cumsum(used.astype(jnp.int32), axis=-1)
    count = sums[..., -1]
    spare = jnp.cumsum((~used).astype(jnp.int32), axis=-1)
    rank = jnp.where(used, sums - 1, count[..., None] + spare - 1)
    hot = rank[..., None, :] == jnp.arange(slots, dtype=jnp.int32)[:, None]
    entry = jnp.sum(jnp.where(hot, entry[..., None, :], 0), axis=-1, dtype=jnp.int32)
    most = jnp.max(count, axis=-1).astype(jnp.int32)
    code_blk = jnp.concatenate([codes.reshape(blocks, BLK)] * (LANES // BLK), axis=1)
    code_key = jnp.concatenate([codes, jnp.full((BLK,), -1, jnp.int32)])
    code_key = jnp.broadcast_to(code_key[:, None], (length + BLK, LANES))
    return [(entry[i], most[i], code_key, code_blk) for i in range(layers)]


def dot_nt(left, right):
    return lax.dot_general(left, right, (((1,), (1,)), ((), ())), preferred_element_type=F32)


def dot_nn(left, right):
    return lax.dot_general(left, right, (((1,), (0,)), ((), ())), preferred_element_type=F32)


def dot_tn(left, right):
    return lax.dot_general(left, right, (((0,), (0,)), ((), ())), preferred_element_type=F32)


def first_head(rows):
    return lax.broadcasted_iota(jnp.int32, (rows, LANES), 1) < BLK


def stacked(value, first):
    zero = jnp.zeros_like(value)
    return jnp.concatenate([jnp.where(first, value, zero), jnp.where(first, zero, value)], axis=0)


def block_rows(block):
    return pl.ds(pl.multiple_of(block * BLK, BLK), BLK)


def slot_entries(slot_ref, pair, block, count):
    words = [slot_ref[pair, block - 1, s] for s in range(count)]
    return [(word & 255, (word >> 8) & 255, word >> 16) for word in words]


def picked(ref, entries):
    return jnp.concatenate([ref[block_rows(entry[0]), :] for entry in entries], axis=0)


def visible(code_key_ref, code_row, entries):
    first = first_head(1)
    pieces = []
    for _, place, which in entries:
        row = jnp.where((which == 1) & ~first | (which == 2) & first, -2, code_row)
        pieces.append(code_key_ref[block_rows(place), :] == row)
    return jnp.concatenate(pieces, axis=0)


def middle_blocks(blocks, slots, most, work):
    small = min(SMALL_SLOTS, slots)

    @pl.when(most <= small)
    def _():
        for block in range(1, blocks - 1):
            work(block, small)

    @pl.when(most > small)
    def _():
        def body(block, carry):
            work(block, slots)
            return carry

        lax.fori_loop(1, blocks - 1, body, 0, unroll=2)


def forward_kernel(slot_ref, most_ref, q_ref, k_ref, v_ref, code_key_ref, code_blk_ref, out_ref, lse_ref, *, scale):
    pair = pl.program_id(0)
    blocks = q_ref.shape[0] // BLK
    first = first_head(BLK)

    def rows(taken, keys, values, mask):
        query = [stacked(q_ref[block_rows(block), :] * jnp.asarray(scale, BF16), first) for block in taken]
        query = jnp.concatenate(query, axis=0)
        scores = jnp.where(mask, dot_nt(keys, query), MASKED_SCORE)
        top = jnp.max(scores, axis=0, keepdims=True)
        weights = jnp.exp(scores - top)
        total = jnp.sum(weights, axis=0, keepdims=True)
        mixed = dot_tn((weights * (1.0 / total)).astype(BF16), values)
        log_sum = top + jnp.log(total)
        for turn, block in enumerate(taken):
            part = mixed[turn * LANES : (turn + 1) * LANES]
            out_ref[block_rows(block), :] = jnp.where(first, part[:BLK], part[BLK:]).astype(BF16)
            lse_ref[0, pl.ds(block, 1), :] = log_sum[:, turn * LANES : (turn + 1) * LANES]

    edges = (0, blocks - 1)
    mask = [code_key_ref[0 : blocks * BLK, :] == code_blk_ref[pl.ds(block, 1), :] for block in edges]
    rows(edges, k_ref[...], v_ref[...], jnp.concatenate(mask, axis=1))

    def work(block, count):
        entries = slot_entries(slot_ref, pair, block, count)
        mask = visible(code_key_ref, code_blk_ref[pl.ds(block, 1), :], entries)
        rows((block,), picked(k_ref, entries), picked(v_ref, entries), mask)

    middle_blocks(blocks, slot_ref.shape[2], most_ref[pair], work)


def backward_kernel(
    slot_ref,
    most_ref,
    q_ref,
    k_ref,
    v_ref,
    mixed_ref,
    grad_ref,
    lse_ref,
    code_key_ref,
    code_blk_ref,
    out_ref,
    dk_ref,
    dv_ref,
    *,
    scale,
    start,
):
    step = pl.program_id(0)
    pair = step + start
    blocks = q_ref.shape[0] // BLK
    width = out_ref.shape[1] // 3
    first = first_head(BLK)
    ones = jnp.ones((8, LANES), F32)

    def column(kind):
        return pl.ds(pl.multiple_of(kind * width + step * LANES, LANES), LANES)

    def rows(taken, keys, values, mask):
        query, grad, along = [], [], []
        for block in taken:
            at = block_rows(block)
            query.append(stacked(q_ref[at, :] * jnp.asarray(scale, BF16), first))
            grad.append(stacked(grad_ref[at, :], first))
            along.append(grad[-1].astype(F32) * jnp.concatenate([mixed_ref[at, :].astype(F32)] * 2, axis=0))
        query, grad, along = [jnp.concatenate(part, axis=0) for part in (query, grad, along)]
        along = lax.dot_general(
            ones, along, (((1,), (1,)), ((), ())), precision=lax.Precision.HIGHEST, preferred_element_type=F32
        )[0:1]
        lse = jnp.concatenate([lse_ref[0, pl.ds(block, 1), :] for block in taken], axis=1)
        prob = jnp.where(mask, jnp.exp(dot_nt(keys, query) - lse), 0.0)
        slope = (prob * (dot_nt(values, grad) - along)).astype(BF16)
        back = dot_tn(keys, slope).T
        for turn, block in enumerate(taken):
            part = back[turn * LANES : (turn + 1) * LANES]
            out_ref[block_rows(block), column(0)] = (jnp.where(first, part[:BLK], part[BLK:]) * scale).astype(BF16)
        return dot_nn(slope, query), dot_nn(prob.astype(BF16), grad)

    edges = (0, blocks - 1)
    mask = [code_key_ref[0 : blocks * BLK, :] == code_blk_ref[pl.ds(block, 1), :] for block in edges]
    dk, dv = rows(edges, k_ref[...], v_ref[...], jnp.concatenate(mask, axis=1))
    dk_ref[...] = dk
    dv_ref[...] = dv

    def work(block, count):
        entries = slot_entries(slot_ref, pair, block, count)
        mask = visible(code_key_ref, code_blk_ref[pl.ds(block, 1), :], entries)
        dk, dv = rows((block,), picked(k_ref, entries), picked(v_ref, entries), mask)
        for s, entry in enumerate(entries):
            at = block_rows(entry[0])
            dk_ref[at, :] += dk[s * BLK : (s + 1) * BLK]
            dv_ref[at, :] += dv[s * BLK : (s + 1) * BLK]

    middle_blocks(blocks, slot_ref.shape[2], most_ref[pair], work)
    out_ref[:, column(1)] = dk_ref[...].astype(BF16)
    out_ref[:, column(2)] = dv_ref[...].astype(BF16)


def whole_block(shape):
    return pl.BlockSpec(shape, lambda p, *_: (0,) * len(shape))


def attend_forward(project_low, tables, scale):
    entry, most, code_key, code_blk = tables
    length = project_low.shape[0]
    pairs = project_low.shape[1] // (3 * LANES)
    blocks = length // BLK

    def column(kind):
        return pl.BlockSpec((length, LANES), lambda p, *_: (0, kind * pairs + p))

    return pl.pallas_call(
        partial(forward_kernel, scale=scale),
        grid_spec=pltpu.PrefetchScalarGridSpec(
            num_scalar_prefetch=2,
            grid=(pairs,),
            in_specs=[column(0), column(1), column(2), whole_block(code_key.shape), whole_block(code_blk.shape)],
            out_specs=[column(0), pl.BlockSpec((1, blocks, LANES), lambda p, *_: (p, 0, 0))],
        ),
        out_shape=[
            jax.ShapeDtypeStruct((length, pairs * LANES), BF16),
            jax.ShapeDtypeStruct((pairs, blocks, LANES), F32),
        ],
        compiler_params=pltpu.CompilerParams(vmem_limit_bytes=VMEM_LIMIT),
    )(entry, most, project_low, project_low, project_low, code_key, code_blk)


def attend_backward(project_low, mixed, grad_mixed, lse, tables, scale, start, stop):
    entry, most, code_key, code_blk = tables
    length = project_low.shape[0]
    pairs = project_low.shape[1] // (3 * LANES)
    blocks = length // BLK
    shape = (length, 3 * (stop - start) * LANES)

    def column(kind):
        return pl.BlockSpec((length, LANES), lambda p, *_: (0, kind * pairs + p + start))

    return pl.pallas_call(
        partial(backward_kernel, scale=scale, start=start),
        grid_spec=pltpu.PrefetchScalarGridSpec(
            num_scalar_prefetch=2,
            grid=(stop - start,),
            in_specs=[
                column(0),
                column(1),
                column(2),
                column(0),
                column(0),
                pl.BlockSpec((1, blocks, LANES), lambda p, *_: (p + start, 0, 0)),
                whole_block(code_key.shape),
                whole_block(code_blk.shape),
            ],
            out_specs=whole_block(shape),
            scratch_shapes=[pltpu.VMEM((length, LANES), F32), pltpu.VMEM((length, LANES), F32)],
        ),
        out_shape=jax.ShapeDtypeStruct(shape, BF16),
        compiler_params=pltpu.CompilerParams(vmem_limit_bytes=VMEM_LIMIT),
    )(entry, most, project_low, project_low, project_low, mixed, grad_mixed, lse, code_key, code_blk)


class Weight:
    def __init__(self, own, layer, fetch, axis):
        self.axis, self.bit = axis, fetch.bit
        self.arrays = [own] + fetch.pieces
        rows, columns = own.shape[-2:]
        self.shape = (2 * rows, columns) if axis == 0 else (rows, 2 * columns)
        if own.ndim == 3:
            own_spec = pl.BlockSpec((1, rows, columns), lambda i: (layer, 0, 0))
        else:
            own_spec = whole_block(own.shape)
        self.specs = [own_spec] + [whole_block(piece.shape) for piece in fetch.pieces]

    def assemble(self, refs, place, into):
        own = refs[0]
        rows, columns = own.shape[-2:]
        into[0:rows, 0:columns] = own[0] if len(own.shape) == 3 else own[...]
        base = rows if self.axis == 0 else 0
        lanes = pl.ds(0 if self.axis == 0 else columns, columns)
        if self.bit is None:
            into[base : base + rows, lanes] = refs[1][...]
            return
        half = rows // 2
        place = (place >> self.bit) & 1
        into[pl.ds(pl.multiple_of(base + place * half, half), half), lanes] = refs[1][...]
        into[pl.ds(pl.multiple_of(base + (1 - place) * half, half), half), lanes] = refs[2][...]


def token_kernel(work, inputs, weights, outputs, place, length):
    block = min(TOKEN_BLOCK, length)
    in_specs, arrays = [pl.BlockSpec(memory_space=pltpu.SMEM)], [place]
    for item in inputs:
        if not isinstance(item, tuple):
            item = (ROWS, item, 0)
        array = item[1]
        if item[0] == WHOLE:
            in_specs.append(whole_block(array.shape))
        else:
            in_specs.append(pl.BlockSpec((block, array.shape[1]), lambda i, skip=item[2] // block: (i + skip, 0)))
        arrays.append(array)
    counts = []
    for weight in weights:
        in_specs += weight.specs
        arrays += weight.arrays
        counts.append(len(weight.arrays))
    out_specs, out_shapes = [], []
    for out in outputs:
        if out[0] == SUM:
            out_specs.append(whole_block(out[1:]))
            out_shapes.append(jax.ShapeDtypeStruct(out[1:], F32))
        else:
            out_specs.append(pl.BlockSpec((block, out[0]), lambda i: (i, 0)))
            out_shapes.append(jax.ShapeDtypeStruct((length, out[0]), out[1]))

    def kernel(*refs):
        place_ref, refs = refs[0], refs[1:]
        ins, refs = refs[: len(inputs)], refs[len(inputs) :]
        parts = []
        for count in counts:
            parts.append(refs[:count])
            refs = refs[count:]
        outs, scratch = refs[: len(outputs)], refs[len(outputs) :]
        step = pl.program_id(0)

        @pl.when(step == 0)
        def _():
            for weight, part, into in zip(weights, parts, scratch):
                weight.assemble(part, place_ref[0, 0], into)
            for out, ref in zip(outputs, outs):
                if out[0] == SUM:
                    ref[...] = jnp.zeros_like(ref)

        work(ins, scratch, outs)

    return pl.pallas_call(
        kernel,
        grid=(length // block,),
        in_specs=in_specs,
        out_specs=out_specs,
        out_shape=out_shapes,
        scratch_shapes=[pltpu.VMEM(weight.shape, BF16) for weight in weights],
        compiler_params=pltpu.CompilerParams(vmem_limit_bytes=VMEM_LIMIT),
    )(*arrays)


def normed_of(value):
    mean = jnp.mean(value, axis=1, keepdims=True)
    centered = value - mean
    variance = jnp.mean(centered * centered, axis=1, keepdims=True)
    inverse = lax.rsqrt(variance + EPSILON)
    return centered * inverse, inverse


def norm_grad(grad_out, normed, inverse, gain):
    scaled = grad_out * gain
    mean = jnp.mean(scaled, axis=1, keepdims=True)
    along = jnp.mean(scaled * normed, axis=1, keepdims=True)
    return inverse * (scaled - mean - normed * along)


def add_rows(ref, *terms):
    for row, term in enumerate(terms):
        ref[row : row + 1, :] += jnp.sum(term, axis=0, keepdims=True)


def both(refs):
    count = len(refs) // 2
    return joined(refs[:count]).astype(F32) + joined(refs[count:]).astype(F32)


def joined(refs):
    return jnp.concatenate([ref[...] for ref in refs], axis=1) if len(refs) > 1 else refs[0][...]


def put_halves(refs, value):
    half = value.shape[1] // 2
    refs[0][...] = value[:, :half].astype(refs[0].dtype)
    refs[1][...] = value[:, half:].astype(refs[1].dtype)


def project_kernel(ins, weights, outs):
    outs[0][...] = (dot_nn(joined(ins[:2]), weights[0][...]) + ins[2][...]).astype(BF16)


def norm_project_kernel(layer, ins, weights, outs):
    first_ref, vec_ref, bias_ref = ins[4:]
    vec_ref = vec_ref.at[layer]
    hidden_ref, low_own_ref, low_other_ref, hat_ref, inverse_ref, project_ref = outs
    normed, inverse = normed_of(first_ref[...] + (both(ins[:4]) + vec_ref[0:1, :]))
    hidden = normed * vec_ref[1:2, :] + vec_ref[2:3, :]
    hidden_ref[...] = hidden
    low = hidden.astype(BF16)
    put_halves((low_own_ref, low_other_ref), low)
    hat_ref[...] = normed.astype(BF16)
    inverse_ref[...] = inverse
    project_ref[...] = (dot_nn(low, weights[0][...]) + bias_ref[...]).astype(BF16)


def product_kernel(ins, weights, outs):
    put_halves(outs, dot_nn(ins[0][...], weights[0][...]))


def feed_forward_kernel(layer, ins, weights, outs):
    vec_ref, bias_ref = ins[4:6]
    vec_ref = vec_ref.at[layer]
    first_ref, low_ref, hat_ref, inverse_ref, active_ref, slope_ref = outs[2:]
    hidden = joined(ins[6:]).astype(F32)
    normed, inverse = normed_of(hidden + (both(ins[:4]) + vec_ref[0:1, :]))
    first = normed * vec_ref[1:2, :] + vec_ref[2:3, :]
    first_ref[...] = first
    low = first.astype(BF16)
    low_ref[...] = low
    hat_ref[...] = normed.astype(BF16)
    inverse_ref[...] = inverse
    inner = dot_nn(low, weights[0][...]) + bias_ref[...]
    square = inner * inner
    bent = jnp.tanh(GELU_SCALE * inner * (1.0 + GELU_CUBE * square))
    half = 0.5 * (1.0 + bent)
    active = (inner * half).astype(BF16)
    active_ref[...] = active
    slope = half + 0.5 * GELU_SCALE * inner * (1.0 - bent * bent) * (1.0 + 3.0 * GELU_CUBE * square)
    slope_ref[...] = slope.astype(BF16)
    put_halves(outs, dot_nn(active, weights[1][...]))


def loss_kernel(layer, tokens, ins, weights, outs):
    first_ref, vec_ref, goal_own_ref, goal_other_ref, code_ref = ins[4:]
    vec_ref = vec_ref.at[layer]
    grad_ref, hidden_own_ref, hidden_other_ref, low_own_ref, low_other_ref, sums_ref, loss_ref = outs
    normed, inverse = normed_of(first_ref[...] + (both(ins[:4]) + vec_ref[0:1, :]))
    hidden = normed * vec_ref[1:2, :] + vec_ref[2:3, :]
    put_halves((hidden_own_ref, hidden_other_ref), hidden)
    error = hidden - joined((goal_own_ref, goal_other_ref)).astype(F32)
    grad_out = jnp.where(code_ref[:, 0:1] < tokens, error, 0.0)
    grad = norm_grad(grad_out, normed, inverse, vec_ref[1:2, :])
    grad_ref[...] = grad
    low = grad.astype(BF16)
    put_halves((low_own_ref, low_other_ref), low)
    add_rows(sums_ref, grad_out * normed, grad_out, low.astype(F32))
    squares = grad_out * error
    half = squares.shape[1] // 2
    add_rows(loss_ref, squares[:, :half] + squares[:, half:])


def second_norm_kernel(layer, ins, weights, outs):
    base_own_ref, base_other_ref, hat_ref, inverse_ref, vec_ref = ins[2:]
    vec_ref = vec_ref.at[layer]
    grad_ref, low_own_ref, low_other_ref, sums_ref = outs
    normed = hat_ref[...].astype(F32)
    grad_out = joined((base_own_ref, base_other_ref)) + both(ins[:2])
    grad = norm_grad(grad_out, normed, inverse_ref[...], vec_ref[1:2, :])
    grad_ref[...] = grad
    low = grad.astype(BF16)
    put_halves((low_own_ref, low_other_ref), low)
    add_rows(sums_ref, grad_out * normed, grad_out, low.astype(F32))


def feed_backward_kernel(ins, weights, outs):
    low_own_ref, low_other_ref, slope_ref = ins
    part_ref, inner_ref, sums_ref = outs
    low = joined((low_own_ref, low_other_ref))
    inner = (dot_nt(low, weights[0][...]) * slope_ref[...].astype(F32)).astype(BF16)
    inner_ref[...] = inner
    part_ref[...] = dot_nt(inner, weights[1][...]).astype(BF16)
    total = jnp.sum(inner.astype(F32), axis=0, keepdims=True)
    columns = sums_ref.shape[1]
    for row in range(total.shape[1] // columns):
        sums_ref[row : row + 1, :] += total[:, row * columns : (row + 1) * columns]


def first_norm_kernel(layer, ins, weights, outs):
    base_ref, hat_ref, inverse_ref, vec_ref = ins[2:]
    vec_ref = vec_ref.at[layer]
    grad_own_ref, grad_other_ref, low_own_ref, low_other_ref, mixed_ref, sums_ref = outs
    normed = hat_ref[...].astype(F32)
    grad_out = base_ref[...] + both(ins[:2])
    grad = norm_grad(grad_out, normed, inverse_ref[...], vec_ref[1:2, :])
    put_halves((grad_own_ref, grad_other_ref), grad)
    low = grad.astype(BF16)
    put_halves((low_own_ref, low_other_ref), low)
    mixed_ref[...] = dot_nt(low, weights[0][...]).astype(BF16)
    add_rows(sums_ref, grad_out * normed, grad_out, low.astype(F32))


def project_backward_kernel(cuts, ins, weights, outs):
    sums_ref = outs[-1]
    width = weights[0].shape[1] // 3
    part = None
    for ref, start, stop in zip(ins, cuts[:-1], cuts[1:]):
        lanes = (stop - start) * LANES
        sums_ref[0:1, start * LANES : stop * LANES] += jnp.sum(ref[:, 0:lanes].astype(F32), axis=0, keepdims=True)
        for kind in range(3):
            at = kind * width + start * LANES
            term = dot_nt(ref[:, kind * lanes : (kind + 1) * lanes], weights[0][:, at : at + lanes])
            part = term if part is None else part + term
    if len(outs) > 2:
        put_halves(outs, part)
    else:
        outs[0][...] = part.astype(BF16)


def pack_kernel(split_count, *refs):
    own_ref, other_ref = refs[-2:]
    half = own_ref.shape[1]
    for at, ref in enumerate(refs[:-2]):
        rows = slice(8 * at, 8 * at + 8)
        if at < split_count:
            own_ref[rows, :] = ref[:, :half]
            other_ref[rows, :] = ref[:, half:]
        else:
            own_ref[rows, :] = ref[...]
            other_ref[rows, :] = ref[...]


def pack(split_terms, whole_terms):
    half = whole_terms[0].shape[1]
    shape = jax.ShapeDtypeStruct((8 * (len(split_terms) + len(whole_terms)), half), F32)
    return pl.pallas_call(partial(pack_kernel, len(split_terms)), out_shape=[shape, shape])(
        *split_terms, *whole_terms
    )


def unpack_kernel(layers, rows_up, tokens, ref, *outs):
    half = ref.shape[1]
    scale_ref, loss_ref, split_refs, query_ref, up_ref = outs[0], outs[1], outs[2:8], outs[8], outs[9]
    base = 16 * layers
    loss_row, count_row = base + 16 * layers, base + 16 * layers + 8
    count = ref[count_row : count_row + 1, 0:1]
    scale = 2.0 * tokens / count
    scale_ref[...] = jnp.broadcast_to(scale, scale_ref.shape)
    loss = jnp.sum(ref[loss_row : loss_row + 1, :], axis=1, keepdims=True)
    loss_ref[...] = jnp.broadcast_to(loss / (2.0 * half * count), loss_ref.shape)
    for layer in range(layers):
        at = slice(layer, layer + 1)
        for term in range(6):
            row = 16 * layer + 8 * (term // 3) + term % 3
            split_refs[term][at, :] = ref[row : row + 1, :] * scale
        row = base + 16 * layer
        query_ref[at, :] = ref[row : row + 1, :] * scale
        for part in range(rows_up):
            up_ref[at, part * half : (part + 1) * half] = ref[row + 8 + part : row + 9 + part, :] * scale


def unpack(terms, layers, feed, tokens):
    half = terms.shape[1]
    shapes = [(8, LANES), (8, LANES)] + [(layers, half)] * 7 + [(layers, feed)]
    return pl.pallas_call(
        partial(unpack_kernel, layers, feed // half, tokens),
        out_shape=[jax.ShapeDtypeStruct(shape, F32) for shape in shapes],
    )(terms)


def cross(block, pairs):
    return lax.ppermute(block, (ROW, COL), pairs)


def from_partner(block):
    both_blocks = lax.all_gather(block, COL)
    return lax.dynamic_index_in_dim(both_blocks, 1 - lax.axis_index(COL), 0, keepdims=False)


class Sequence:
    def __init__(self, block):
        self.block, self.got = block, cross(block, [(1, 0), (2, 3)])

    def pass_on(self, line):
        self.got = line.mark(line.next(self.got))
        self.sent = [cross(part, [(0, 2), (3, 1)]) for part in (line.next(self.block), self.got)]

    def halves(self):
        keeps = lax.axis_index(ROW) == lax.axis_index(COL)
        return [jnp.where(keeps, mine, sent) for mine, sent in zip((self.block, self.got), self.sent)]


def finish_kernel(layers, place_ref, scale_ref, *refs):
    step = pl.program_id(0)
    outs = refs[2 * layers :]
    scale = scale_ref[0:1, 0:1]
    for at in range(2 * layers):

        @pl.when(step == at)
        def _():
            value = refs[at][...].astype(F32) * scale
            start = 0
            for out in outs:
                columns = out.shape[-1]
                if len(out.shape) == 3:
                    out[0] = value[:, start : start + columns]
                    start += columns
                else:
                    for kind in range(out.shape[2]):
                        out[0, :, kind, :] = value[:, start : start + columns]
                        start += columns


def finish(halves, outputs, place, scale, work=None):
    layers = LAYERS
    arrays, in_specs, rows = [], [whole_block(scale.shape)], None
    for array in [half for pair in halves for half in pair]:
        rows = array.shape[0]
        in_specs.append(whole_block(array.shape))
        arrays.append(array)

    def out_spec(shape):
        zeros = (0,) * len(shape)
        return pl.BlockSpec((1, rows) + shape, lambda i, place_ref: (i // 2, ((place_ref[0, 0] & 1) + i) % 2) + zeros)

    return pl.pallas_call(
        work or partial(finish_kernel, layers),
        grid_spec=pltpu.PrefetchScalarGridSpec(
            num_scalar_prefetch=1,
            grid=(2 * layers,),
            in_specs=in_specs,
            out_specs=[out_spec(shape) for shape in outputs],
        ),
        out_shape=[jax.ShapeDtypeStruct((layers, 2 * rows) + shape, F32) for shape in outputs],
        compiler_params=pltpu.CompilerParams(vmem_limit_bytes=VMEM_LIMIT),
    )(place, scale, *arrays)


def finish_qkv_kernel(cuts, place_ref, scale_ref, *refs):
    step = pl.program_id(0)
    out_ref, query_key_ref, value_ref = refs[-3:]
    scale = scale_ref[0:1, 0:1]
    half = out_ref.shape[2]
    parts = refs[:-3]
    for layer, layer_cuts in enumerate(cuts):
        pieces, parts = parts[: 2 * len(layer_cuts) - 2], parts[2 * len(layer_cuts) - 2 :]
        for side in range(2):

            @pl.when(step == 2 * layer + side)
            def _():
                for turn, (start, stop) in enumerate(zip(layer_cuts[:-1], layer_cuts[1:])):
                    value = pieces[2 * turn + side][...].astype(F32) * scale
                    if start == 0:
                        out_ref[0] = value[:, :half]
                        value = value[:, half:]
                    width = (stop - start) * LANES
                    columns = slice(start * LANES, stop * LANES)
                    query_key_ref[0, :, 0, columns] = value[:, :width]
                    query_key_ref[0, :, 1, columns] = value[:, width : 2 * width]
                    value_ref[0, :, columns] = value[:, 2 * width :]


def body(
    tokens_in,
    teacher,
    qkv_weight,
    query_bias,
    out_weight,
    out_bias,
    first_gain,
    first_shift,
    up_weight,
    up_bias,
    down_weight,
    down_bias,
    second_gain,
    second_shift,
    random_blocks,
    segment_ids,
    padding_mask,
):
    row_count = lax.axis_size(ROW)
    layers, half, _, inner = qkv_weight.shape
    width = 2 * half
    feed = up_weight.shape[2]
    length = segment_ids.shape[1]
    heads_local = random_blocks.shape[1] // row_count
    head_width = inner // heads_local
    scale = head_width ** (-0.5)
    pairs = inner // LANES
    keeps = lax.axis_index(ROW) == lax.axis_index(COL)
    mine = lax.axis_index(COL)
    place = lax.axis_index(DP).astype(jnp.int32).reshape(1, 1)
    line = Line()

    stacks = {QKV: qkv_weight, OUT: out_weight, UP: up_weight, DOWN: down_weight}
    fetch, shard = {}, {}

    def ask(layer, name, bit):
        if layer < layers:
            fetch[layer, name] = Fetch(line, stacks[name], layer, bit)

    def pass_on(layer, name):
        if layer < layers:
            fetch[layer, name].pass_on(line)

    def arrived(layer, *names):
        if layer < layers:
            for name in names:
                fetch[layer, name].arrived(line)

    def weight(layer, name):
        own = shard[layer] if name == QKV else stacks[name]
        return Weight(own, layer, fetch[layer, name], 1 if name in (OUT, DOWN) else 0)

    def kernel(work, inputs, weights, outputs, main=0):
        first = inputs[0]
        first = (first[0], line.next(first[1])) + first[2:] if isinstance(first, tuple) else line.next(first)
        outs = token_kernel(work, [first] + inputs[1:], weights, outputs, place, length)
        line.mark(outs[main])
        return outs

    tokens = Sequence(tokens_in)
    ask(0, QKV, 0)
    ask(0, DOWN, 1)
    ask(0, UP, 0)
    vectors = jnp.stack([out_bias, first_gain, first_shift, down_bias, second_gain, second_shift])
    line.mark(line.last[0], vectors)
    shard[0] = line.mark(line.next(qkv_weight[0]).reshape(half, 3 * inner))
    segment = lax.dynamic_index_in_dim(segment_ids, mine, 0, keepdims=False)
    valid = lax.dynamic_index_in_dim(padding_mask, mine, 0, keepdims=False)
    local_blocks = lax.dynamic_slice_in_dim(random_blocks, lax.axis_index(ROW) * heads_local, heads_local, 1)
    tables = attention_tables(line.next(segment), valid, local_blocks, LANES // head_width)
    line.mark(*[part for table in tables for part in table])
    pass_on(0, QKV)
    tokens.pass_on(line)
    arrived(0, QKV)
    pass_on(0, DOWN)
    tokens_low = tokens.halves()

    halves_out = [(half, BF16), (half, BF16)]

    def swap_row(part):
        return [swap(piece, ROW) for piece in part]

    saved = []
    for layer in range(layers):
        w = {QKV: weight(layer, QKV)}
        bias = jnp.concatenate([query_bias[layer], jnp.zeros((2 * inner,), F32)])[None]
        hidden_hat = hidden_inverse = None
        if layer == 0:
            hidden = hidden_low = tokens_low
            (project_low,) = kernel(project_kernel, hidden + [(WHOLE, bias)], [w[QKV]], [(3 * inner, BF16)])
            ask(0, OUT, None)
            vectors = jnp.concatenate([vectors, swap(vectors, COL)], axis=2)
            first_vec, second_vec = vectors[:3].transpose(1, 0, 2), vectors[3:].transpose(1, 0, 2)
            ask(1, QKV, 0)
            pass_on(0, UP)
            ask(1, OUT, 1)
        else:
            hidden, low_own, low_other, hidden_hat, hidden_inverse, project_low = kernel(
                partial(norm_project_kernel, layer - 1),
                [*part, *got, first, (WHOLE, second_vec), (WHOLE, bias)],
                [w[QKV]],
                [(width, F32), (half, BF16), (half, BF16), (width, BF16), (1, F32), (3 * inner, BF16)],
                main=5,
            )
            hidden, hidden_low = [hidden], (low_own, low_other)
            if layer == 1:
                pass_on(1, UP)
        if layer == layers - 1:
            goal = Sequence(line.next(teacher))
        mixed, lse = attend_forward(line.next(project_low), tables[layer], scale)
        line.mark(mixed)
        arrived(layer, OUT, UP, DOWN)
        if layer == 0:
            pass_on(1, QKV)
            pass_on(1, OUT)
        w[OUT] = weight(layer, OUT)
        part = kernel(product_kernel, [mixed], [w[OUT]], halves_out)
        got = swap_row(part)
        if layer == layers - 1:
            goal.pass_on(line)
        if layer == 0:
            ask(1, UP, 0)
            ask(1, DOWN, None)
            arrived(1, QKV, OUT)
        w[UP], w[DOWN] = weight(layer, UP), weight(layer, DOWN)
        *part, first, first_low, first_hat, first_inverse, active, slope = kernel(
            partial(feed_forward_kernel, layer),
            [*part, *got, (WHOLE, first_vec), (WHOLE, up_bias[layer][None])] + hidden,
            [w[UP], w[DOWN]],
            halves_out + [(width, F32), (width, BF16), (width, BF16), (1, F32), (feed, BF16), (feed, BF16)],
        )
        got = swap_row(part)
        if layer == 0:
            if layers > 1:
                shard[1] = line.mark(line.next(qkv_weight[1]).reshape(half, 3 * inner))
        saved.append(
            SimpleNamespace(
                w=w,
                hidden_low=hidden_low,
                hidden_hat=hidden_hat,
                hidden_inverse=hidden_inverse,
                project_low=project_low,
                mixed=mixed,
                lse=lse,
                first_low=first_low,
                first_hat=first_hat,
                first_inverse=first_inverse,
                active=active,
                slope=slope,
            )
        )

    goal = goal.halves()

    chains = {}

    def steps(*keys):
        for key in keys:
            if key in chains:
                chains[key].step(line)

    def matmul(left, right):
        return line.mark(dot_tn(left, line.next(right)))

    def matmul_low(left, right):
        return line.mark(lax.optimization_barrier(dot_tn(left, line.next(right))).astype(BF16))

    def send_terms(terms, got, turn):
        if turn > dp_bits():
            return terms, got
        terms = line.mark(terms + line.next(got))
        return terms, swap_bit(terms, turn) if turn < dp_bits() else None

    split_terms, whole_terms = [None] * (2 * layers), [None] * (2 * layers)
    all_cuts = [[0, pairs]] * (layers - 1)
    all_cuts = [[0, max(pairs - 1, 1), pairs] if pairs > 1 else [0, pairs]] + all_cuts
    for layer in reversed(range(layers)):
        final, above = layer == 0, layer + 1
        keep, cuts = saved[layer], all_cuts[layer]
        w = keep.w
        if layer == layers - 1:
            grad_second, hidden_own, hidden_other, low_own, low_other, second_sums, loss_sums = kernel(
                partial(loss_kernel, layer, length),
                [*part, *got, first, (WHOLE, second_vec), *goal, (ROWS, tables[0][2], 0)],
                [],
                [(width, F32), (half, F32), (half, BF16), (half, BF16), (half, BF16), (SUM, 8, width), (SUM, 8, half)],
                main=4,
            )
        else:
            grad_second, low_own, low_other, second_sums = kernel(
                partial(second_norm_kernel, layer),
                [part, got, *grad_hidden, saved[above].hidden_hat, saved[above].hidden_inverse, (WHOLE, second_vec)],
                [],
                [(width, F32), (half, BF16), (half, BF16), (SUM, 8, width)],
                main=2,
            )
        chains[layer, DOWN] = Reduce(matmul_low(keep.active, low_other), False)
        steps((above, DOWN), (above, UP), (above, QKV, 0))
        part, grad_inner, up_sums = kernel(
            feed_backward_kernel,
            [low_own, low_other, keep.slope],
            [w[DOWN], w[UP]],
            [(width, BF16), (feed, BF16), (SUM, 8, half)],
        )
        got = swap(part, ROW)
        up_grad = matmul(keep.first_low, grad_inner)
        chains[layer, UP] = Reduce(line.mark(line.next(up_grad[half:]).astype(BF16)), final)
        chains[layer, UP].own = up_grad[:half]
        chains[layer, DOWN].own = matmul(keep.active, low_own)
        steps((above, DOWN), (above, UP))
        *grad_hidden, low_own, low_other, grad_mixed, first_sums = kernel(
            partial(first_norm_kernel, layer),
            [part, got, grad_second, keep.first_hat, keep.first_inverse, (WHOLE, first_vec)],
            [w[OUT]],
            [(half, F32), (half, F32), (half, BF16), (half, BF16), (inner, BF16), (SUM, 8, width)],
            main=4,
        )
        out_other = matmul_low(keep.mixed, low_other)
        out_own = matmul(keep.mixed, low_own)
        split_terms[2 * layer : 2 * layer + 2] = [second_sums, first_sums]
        whole_terms[2 * layer + 1] = up_sums
        steps((above, QKV, 0), (layer, DOWN))
        input_own, input_other = keep.hidden_low
        projects = []
        for start, stop in zip(cuts[:-1], cuts[1:]):
            grad_project = attend_backward(
                keep.project_low, keep.mixed, line.next(grad_mixed), keep.lse, tables[layer], scale, start, stop
            )
            line.mark(grad_project)
            projects.append(grad_project)
            qkv_other = matmul_low(input_other, grad_project)
            if start == 0:
                qkv_other = line.mark(jnp.concatenate([out_other, qkv_other], axis=1))
            chain = chains[layer, QKV, start] = Reduce(qkv_other, final and start == 0)
            if final:
                chain.own = matmul(input_own, grad_project)
                if start == 0:
                    chain.own = jnp.concatenate([out_own, chain.own], axis=1)
                if stop < pairs:
                    steps((1, DOWN), (1, UP), (1, QKV, 0), (0, DOWN), *[(0, QKV, at) for at in range(start)], (0, UP))
            else:
                steps((layer, DOWN), (layer, UP))

        def project_backward():
            return kernel(
                partial(project_backward_kernel, cuts),
                projects,
                [w[QKV]],
                [(half, BF16), (half, BF16), (SUM, 8, inner)] if final else [(width, BF16), (SUM, 8, inner)],
            )

        if not final:
            part, query_sums = project_backward()
            got = swap(part, ROW)
            chain.own = jnp.concatenate([out_own, matmul(input_own, grad_project)], axis=1)
            whole_terms[2 * layer] = query_sums

    down, up, first_pairs, last_pair = (0, DOWN), (0, UP), (0, QKV, 0), (0, QKV, all_cuts[0][-2])

    def finished(halves, outputs, work=None):
        outs = finish([(line.next(own), got) for own, got in halves], outputs, place, scale_block, work)
        line.mark(outs[0])
        return outs

    made = {}

    def make(name, shape):
        if name not in made and all(chains[layer, name].done() for layer in range(layers)):
            (made[name],) = finished([chains[layer, name].halves() for layer in range(layers)], [shape])

    part_own, part_other, whole_terms[0] = project_backward()
    got = swap(jnp.where(keeps, part_own, part_other), ROW)
    steps((1, UP), first_pairs, down, up)
    got = line.next(got).astype(F32)
    grad = jnp.where(keeps, grad_hidden[1] + part_other.astype(F32), grad_hidden[0] + part_own.astype(F32)) + got
    grad_low = line.mark(grad.astype(BF16))
    grad_own, grad_got = swap(grad, ROW), from_partner(grad_low)
    steps((1, QKV, 0), last_pair, first_pairs, up, down)
    count = jnp.sum(padding_mask.astype(F32)) * jnp.full((8, half), 0.5, F32)
    own, other = pack(split_terms, whole_terms + [loss_sums, count])
    terms, terms_got = line.mark(own), swap(other, COL)
    steps(first_pairs, last_pair, (1, QKV, 0))
    grad_own = line.mark(line.next(grad_own))
    terms, terms_got = send_terms(terms, terms_got, 0)
    steps(up, down, last_pair, first_pairs)
    terms, terms_got = send_terms(terms, terms_got, 1)
    steps(up, last_pair, first_pairs)
    terms, terms_got = send_terms(terms, terms_got, 2)
    crossed = from_partner(line.next(hidden_other))
    steps(down)
    for turn in range(3, dp_bits() + 1):
        terms, terms_got = send_terms(terms, terms_got, turn)
    scale_block, loss, *vectors = unpack(terms, layers, feed, float(length * row_count * lax.axis_size(DP)))
    line.mark(scale_block)
    make(DOWN, (half,))
    input_grad = line.mark(jnp.where(keeps, line.next(grad_own), grad_got.astype(F32)) * scale_block[0:1, 0:1])
    hidden_out = line.mark(jnp.where(keeps, line.next(hidden_own), crossed.astype(F32)))
    steps(up)
    make(UP, (feed,))
    steps(last_pair, first_pairs)
    while not all(chain.done() for chain in chains.values()):
        steps(*chains)
    make(DOWN, (half,))
    make(UP, (feed,))
    down_grads, up_grads = made[DOWN], made[UP]
    parts = [chains[layer, QKV, start].halves() for layer in range(layers) for start in all_cuts[layer][:-1]]
    out_grads, query_key_grads, value_grads = finished(
        parts, [(half,), (2, inner), (inner,)], partial(finish_qkv_kernel, all_cuts)
    )
    loss = loss[0, 0]
    second_gain_grad, second_shift_grad, down_bias_grad, first_gain_grad, first_shift_grad, out_bias_grad = vectors[:6]
    return (
        hidden_out,
        loss,
        input_grad,
        query_key_grads,
        value_grads,
        vectors[6],
        out_grads,
        out_bias_grad,
        first_gain_grad,
        first_shift_grad,
        up_grads,
        vectors[7],
        down_grads,
        down_bias_grad,
        second_gain_grad,
        second_shift_grad,
    )


def solution(mesh):
    return jax.shard_map(
        body,
        mesh=mesh,
        in_specs=(
            P((DP, ROW), COL),
            P((DP, ROW), COL),
            P(None, COL, None, ROW),
            P(None, ROW),
            P(None, ROW, COL),
            P(None, COL),
            P(None, COL),
            P(None, COL),
            P(None, COL, ROW),
            P(None, ROW),
            P(None, ROW, COL),
            P(None, COL),
            P(None, COL),
            P(None, COL),
            P(),
            P(DP, None),
            P(DP, None),
        ),
        out_specs=(
            P((DP, ROW), COL),
            P(),
            P((DP, ROW), COL),
            P(None, COL, None, ROW),
            P(None, COL, ROW),
            P(None, ROW),
            P(None, ROW, COL),
            P(None, COL),
            P(None, COL),
            P(None, COL),
            P(None, COL, ROW),
            P(None, ROW),
            P(None, ROW, COL),
            P(None, COL),
            P(None, COL),
            P(None, COL),
        ),
        check_vma=False,
    )
```

profile of v0, /device:TPU:0, one launch (start us, length us, event | category | flops | bytes accessed | tf_op | source)
XLA Modules:
  0.0 542.5 jit_solution(12873377462249370623)
XLA Ops:
  33.4 4.7 collective-permute-start.5
  41.8 6.9 %collective-permute-done.4.refs_6_.refs_5_ = bf16[192,1152]{1,0:T(8,128)(2,1)S(1)} collective-permute-done((bf16[192,1152]{1,0:T(8,128)(2,1)S(1)}, bf16[192,1152]{1,0:T(8,128)(2,1)S(1)}, u32[]{:S(2)}, u32[]{:S(2)}) %collective-permute-start.4) | collective-permute-done | bytes 442400 | tf_op jit(solution)/shard_map/ppermute | solution.py:39
  69.5 12.5 %shard_map.298 = (bf16[1024,384]{1,0:T(8,128)(2,1)S(1)}, f32[3,16,128]{2,1,0:T(8,128)S(1)}) custom-call(s32[3,14,11]{2,1,0:T(8,128)S(1)} %bitcast.165, s32[3]{0:T(128)S(1)} %get-tuple-element.442.most_ref, bf16[1024,1152]{1,0:T(8,128)(2,1)S(1)} %shard_map.297.q_ref.k_ref.v_ref, bf16[1024,1152]{1,0:T(8,128)(2,1)S(1)} %shard_map.297.q_ref.k_ref.v_ref, ...), custom_call_target="tpu_custom_call" | custom-call | tf_op jit(solution)/shard_map/pallas_call | solution.py:358
  93.9 5.9 %collective-permute-done.13.refs_10_.refs_4_ = bf16[192,1152]{1,0:T(8,128)(2,1)S(1)} collective-permute-done((bf16[192,1152]{1,0:T(8,128)(2,1)S(1)}, bf16[192,1152]{1,0:T(8,128)(2,1)S(1)}, u32[]{:S(2)}, u32[]{:S(2)}) %collective-permute-start.13) | collective-permute-done | bytes 442400 | tf_op jit(solution)/shard_map/ppermute | solution.py:39
  102.4 14.1 %shard_map.300 = (bf16[1024,384]{1,0:T(8,128)(2,1)}, bf16[1024,384]{1,0:T(8,128)(2,1)}, f32[1024,768]{1,0:T(8,128)}, bf16[1024,768]{1,0:T(8,128)(2,1)}, bf16[102...) custom-call(s32[1,1]{1,0:T(1,128)} %bitcast.refs_0_.place_ref, ...), custom_call_target="tpu_custom_call" | custom-call | tf_op jit(solution)/shard_map/pallas_call | solution.py:480
  126.5 7.3 %shard_map.301 = (f32[1024,768]{1,0:T(8,128)}, bf16[1024,384]{1,0:T(8,128)(2,1)S(1)}, bf16[1024,384]{1,0:T(8,128)(2,1)S(1)}, bf16[1024,768]{1,0:T(8,128)(2,1)}, ...) custom-call(s32[1,1]{1,0:T(1,128)} %bitcast.refs_0_.place_ref, bf16[1024,384]{1,0:T(8,128)(2,1)} %get-tuple-element.246.refs_1_, ...), custom_call_target="tpu_custom_call" | custom-call | tf_op jit(solution)/shard_map/pallas_call | solution.py:480
  140.2 12.5 %shard_map.302 = (bf16[1024,384]{1,0:T(8,128)(2,1)S(1)}, f32[3,16,128]{2,1,0:T(8,128)S(1)}) custom-call(s32[3,14,11]{2,1,0:T(8,128)S(1)} %bitcast.168, s32[3]{0:T(128)S(1)} %copy-done.96, bf16[1024,1152]{1,0:T(8,128)(2,1)S(1)} %copy-done.2, bf16[1024,1152]{1,0:T(8,128)(2,1)S(1)} %copy-done.2, bf16[1024,1152]{1,0:T(8,128)(2,1)S(1)} %copy-done.2, ...), custom_call_target="tpu_custom_call" | custom-call | tf_op jit(solution)/shard_map/pallas_call | solution.py:358
  152.8 6.1 %collective-permute-done.20.refs_12_.refs_5_ = bf16[1536,384]{1,0:T(8,128)(2,1)} collective-permute-done((bf16[1536,384]{1,0:T(8,128)(2,1)}, bf16[1536,384]{1,0:T(8,128)(2,1)}, u32[]{:S(2)}, u32[]{:S(2)}) %collective-permute-start.20) | collective-permute-done | bytes 1179680 | tf_op jit(solution)/shard_map/ppermute | solution.py:34
  161.5 5.5 %collective-permute-done.22 = bf16[1024,384]{1,0:T(8,128)(2,1)S(1)} collective-permute-done((bf16[1024,384]{1,0:T(8,128)(2,1)S(1)}, bf16[1024,384]{1,0:T(8,128)(2,1)S(1)}, u32[]{:S(2)}, u32[]{:S(2)}) %collective-permute-start.22) | collective-permute-done | bytes 786464 | tf_op jit(solution)/shard_map/ppermute | solution.py:699
  170.6 14.2 %shard_map.304 = (bf16[1024,384]{1,0:T(8,128)(2,1)S(1)}, bf16[1024,384]{1,0:T(8,128)(2,1)S(1)}, f32[1024,768]{1,0:T(8,128)}, bf16[1024,768]{1,0:T(8,128)(2,1)}, ...) custom-call(s32[1,1]{1,0:T(1,128)} %bitcast.refs_0_.place_ref, ...), custom_call_target="tpu_custom_call" | custom-call | tf_op jit(solution)/shard_map/pallas_call | solution.py:480
  188.2 6.8 %shard_map.305 = (f32[1024,768]{1,0:T(8,128)}, f32[1024,384]{1,0:T(8,128)}, bf16[1024,384]{1,0:T(8,128)(2,1)S(1)}, bf16[1024,384]{1,0:T(8,128)(2,1)S(1)}, bf16[1...) custom-call(s32[1,1]{1,0:T(1,128)} %bitcast.refs_0_.place_ref, ...), custom_call_target="tpu_custom_call" | custom-call | tf_op jit(solution)/shard_map/pallas_call | solution.py:480
  197.9 9.7 %shard_map.306 = (bf16[1024,768]{1,0:T(8,128)(2,1)}, bf16[1024,1536]{1,0:T(8,128)(2,1)}, f32[8,384]{1,0:T(8,128)S(1)}) custom-call(s32[1,1]{1,0:T(1,128)} %bitcast.refs_0_.place_ref, bf16[1024,384]{1,0:T(8,128)(2,1)S(1)} %get-tuple-element.280.refs_1_, bf16[1024,384]{1,0:T(8,128)(2,1)S(1)} %get-tuple-element.272.refs_2_, ...), custom_call_target="tpu_custom_call" | custom-call | tf_op jit(solution)/shard_map/pallas_call | solution.py:480
  209.3 5.0 fusion.30
  219.6 5.9 %shard_map.307 = (f32[1024,384]{1,0:T(8,128)S(1)}, f32[1024,384]{1,0:T(8,128)}, bf16[1024,384]{1,0:T(8,128)(2,1)S(1)}, bf16[1024,384]{1,0:T(8,128)(2,1)S(1)}, bf...) custom-call(s32[1,1]{1,0:T(1,128)} %bitcast.refs_0_.place_ref, bf16[1024,768]{1,0:T(8,128)(2,1)} %get-tuple-element.281.refs_1_, ...), custom_call_target="tpu_custom_call" | custom-call | tf_op jit(solution)/shard_map/pallas_call | solution.py:480
  228.3 8.7 %collective-permute-done.30 = bf16[1536,384]{1,0:T(8,128)(2,1)} collective-permute-done((bf16[1536,384]{1,0:T(8,128)(2,1)}, bf16[1536,384]{1,0:T(8,128)(2,1)}, u32[]{:S(2)}, u32[]{:S(2)}) %collective-permute-start.30) | collective-permute-done | bytes 1179680 | tf_op jit(solution)/shard_map/ppermute | solution.py:34
  240.0 25.4 %shard_map.308.refs_1_ = bf16[1024,1152]{1,0:T(8,128)(2,1)S(1)} custom-call(s32[3,14,11]{2,1,0:T(8,128)S(1)} %bitcast.169, s32[3]{0:T(128)S(1)} %copy-done.97, bf16[1024,1152]{1,0:T(8,128)(2,1)} %get-tuple-element.251.q_ref.k_ref.v_ref, bf16[1024,1152]{1,0:T(8,128)(2,1)} %get-tuple-element.251.q_ref.k_ref.v_ref, ...), custom_call_target="tpu_custom_call" | custom-call | tf_op jit(solution)/shard_map/pallas_call | solution.py:384
  271.9 4.3 shard_map.309
  287.4 5.7 %shard_map.310 = (f32[1024,768]{1,0:T(8,128)}, bf16[1024,384]{1,0:T(8,128)(2,1)S(1)}, bf16[1024,384]{1,0:T(8,128)(2,1)S(1)}, f32[8,768]{1,0:T(8,128)S(1)}) custom-call(s32[1,1]{1,0:T(1,128)} %bitcast.refs_0_.place_ref, bf16[1024,768]{1,0:T(8,128)(2,1)} %get-tuple-element.301.refs_1_, bf16[1024,768]{1,0:T(8,128)(2,1)} %collective-permute-done.33.refs_2_, ...), custom_call_target="tpu_custom_call" | custom-call | tf_op jit(solution)/shard_map/pallas_call | solution.py:480
  293.2 5.0 fusion.36
  309.1 9.3 %shard_map.311 = (bf16[1024,768]{1,0:T(8,128)(2,1)S(1)}, bf16[1024,1536]{1,0:T(8,128)(2,1)}, f32[8,384]{1,0:T(8,128)S(1)}) custom-call(s32[1,1]{1,0:T(1,128)} %bitcast.refs_0_.place_ref, bf16[1024,384]{1,0:T(8,128)(2,1)S(1)} %get-tuple-element.320.refs_1_, bf16[1024,384]{1,0:T(8,128)(2,1)S(1)} %get-tuple-element.309.refs_2_, ...), custom_call_target="tpu_custom_call" | custom-call | tf_op jit(solution)/shard_map/pallas_call | solution.py:480
  318.4 5.0 fusion.37
  338.9 6.4 %shard_map.312 = (f32[1024,384]{1,0:T(8,128)S(1)}, f32[1024,384]{1,0:T(8,128)}, bf16[1024,384]{1,0:T(8,128)(2,1)S(1)}, bf16[1024,384]{1,0:T(8,128)(2,1)S(1)}, bf...) custom-call(s32[1,1]{1,0:T(1,128)} %bitcast.refs_0_.place_ref, bf16[1024,768]{1,0:T(8,128)(2,1)} %copy-done.40, ...), custom_call_target="tpu_custom_call" | custom-call | tf_op jit(solution)/shard_map/pallas_call | solution.py:480
  356.0 17.2 %shard_map.313.refs_1_ = bf16[1024,768]{1,0:T(8,128)(2,1)S(1)} custom-call(s32[3,14,11]{2,1,0:T(8,128)S(1)} %bitcast.166, s32[3]{0:T(128)S(1)} %get-tuple-element.442.most_ref, bf16[1024,1152]{1,0:T(8,128)(2,1)S(1)} %shard_map.297.q_ref.k_ref.v_ref, bf16[1024,1152]{1,0:T(8,128)(2,1)S(1)} %shard_map.297.q_ref.k_ref.v_ref, ...), custom_call_target="tpu_custom_call" | custom-call | tf_op jit(solution)/shard_map/pallas_call | solution.py:384
  394.0 8.7 %shard_map.314.refs_2_ = bf16[1024,384]{1,0:T(8,128)(2,1)S(1)} custom-call(s32[3,14,11]{2,1,0:T(8,128)S(1)} %bitcast.167, s32[3]{0:T(128)S(1)} %get-tuple-element.442.most_ref, bf16[1024,1152]{1,0:T(8,128)(2,1)S(1)} %shard_map.297.q_ref.k_ref.v_ref, bf16[1024,1152]{1,0:T(8,128)(2,1)S(1)} %shard_map.297.q_ref.k_ref.v_ref, ...), custom_call_target="tpu_custom_call" | custom-call | tf_op jit(solution)/shard_map/pallas_call | solution.py:384
  441.9 10.4 %collective-permute-done.58 = bf16[96,1152]{1,0:T(8,128)(2,1)S(1)} collective-permute-done((bf16[96,1152]{1,0:T(8,128)(2,1)S(1)}, bf16[96,1152]{1,0:T(8,128)(2,1)S(1)}, u32[]{:S(2)}, u32[]{:S(2)}) %collective-permute-start.58) | collective-permute-done | bytes 221216 | tf_op jit(solution)/shard_map/ppermute | solution.py:39
  457.8 8.6 %collective-permute-done.63 = bf16[768,384]{1,0:T(8,128)(2,1)S(1)} collective-permute-done((bf16[768,384]{1,0:T(8,128)(2,1)}, bf16[768,384]{1,0:T(8,128)(2,1)S(1)}, u32[]{:S(2)}, u32[]{:S(2)}) %collective-permute-start.63) | collective-permute-done | bytes 589856 | tf_op jit(solution)/shard_map/ppermute | solution.py:39
  476.1 4.8 collective-permute-done.65.refs_1_
  486.1 4.0 collective-permute-done.70
  491.0 3.9 collective-permute-done.68
  519.6 4.6 all-gather.7.cloned.1.call-done
  527.2 3.9 shard_map.319
  531.1 4.3 shard_map.320
  (586 shorter events, 268.5 us)
Async XLA Ops:
  7.2 507.7 %all-gather.5.cloned.1.call-start = ((), (), s32[]{:S(2)}) async-start(), calls=%async_computation | async-start | bytes 2359296 | tf_op jit(solution)/shard_map/all_gather | solution.py:703
  39.7 22.1 %collective-permute-start.6 = (bf16[192,1536]{1,0:T(8,128)(2,1)}, bf16[192,1536]{1,0:T(8,128)(2,1)}, u32[]{:S(2)}, u32[]{:S(2)}) collective-permute-start(bf16[192,1536]{1,0:T(8,128)(2,1)} %dynamic-slice_bitcast_fusion.1), channel_id=1, source_target_pairs={{0,1},{1,0},{2,3},{3,2},{4,5},{5,4},{6,7},{7,6},{8,9},{9,8},{10,11... | collective-permute-start | bytes 1769480 | tf_op jit(solution)/shard_map/ppermute | solution.py:34
  61.8 20.8 %collective-permute-start.10 = (bf16[192,1536]{1,0:T(8,128)(2,1)}, bf16[192,1536]{1,0:T(8,128)(2,1)}, u32[]{:S(2)}, u32[]{:S(2)}) collective-permute-start(bf16[192,1536]{1,0:T(8,128)(2,1)} %collective-permute-done.6.refs_10_.refs_8_), channel_id=1, source_target_pairs={{0,4},{4,0},{8,12},{12,8},{16,20},{20,16},{24,28},{28,24},{1,5},{5... | collective-permute-start | bytes 1769480 | tf_op jit(solution)/shard_map/ppermute | solution.py:39
  65.0 21.0 %collective-permute-start.16 = (f32[6,2,384]{2,0,1:T(8,128)}, f32[6,2,384]{2,0,1:T(8,128)}, u32[]{:S(2)}, u32[]{:S(2)}) collective-permute-start(f32[6,2,384]{2,0,1:T(8,128)} %stack.34), channel_id=1, source_target_pairs={{0,1},{1,0},{2,3},{3,2},{4,5},{5,4},{6,7},{7,6},{8,9},{9,8},{10,11... | collective-permute-start | bytes 55304 | tf_op jit(solution)/shard_map/ppermute | solution.py:34
  119.6 39.3 %collective-permute-start.20 = (bf16[1536,384]{1,0:T(8,128)(2,1)}, bf16[1536,384]{1,0:T(8,128)(2,1)}, u32[]{:S(2)}, u32[]{:S(2)}) collective-permute-start(bf16[1536,384]{1,0:T(8,128)(2,1)} %slice_bitcast_fusion), channel_id=1, source_target_pairs={{0,1},{1,0},{2,3},{3,2},{4,5},{5,4},{6,7},{7,6},{8,9},{9,8},{10,11... | collective-permute-start | bytes 3538952 | tf_op jit(solution)/shard_map/ppermute | solution.py:34
  137.3 29.8 %collective-permute-start.22 = (bf16[1024,384]{1,0:T(8,128)(2,1)S(1)}, bf16[1024,384]{1,0:T(8,128)(2,1)S(1)}, u32[]{:S(2)}, u32[]{:S(2)}) collective-permute-start(bf16[1024,384]{1,0:T(8,128)(2,1)S(1)} %copy-done.121), channel_id=1, source_target_pairs={{1,0},{2,3},{5,4},{6,7},{9,8},{10,11},{13,12},{14,15},{17,16},{18,... | collective-permute-start | bytes 2359304 | tf_op jit(solution)/shard_map/ppermute | solution.py:699
  207.9 29.1 %collective-permute-start.30 = (bf16[1536,384]{1,0:T(8,128)(2,1)}, bf16[1536,384]{1,0:T(8,128)(2,1)}, u32[]{:S(2)}, u32[]{:S(2)}) collective-permute-start(bf16[1536,384]{1,0:T(8,128)(2,1)} %fusion.29), channel_id=1, source_target_pairs={{0,1},{1,0},{2,3},{3,2},{4,5},{5,4},{6,7},{7,6},{8,9},{9,8},{10,11... | collective-permute-start | bytes 3538952 | tf_op jit(solution)/shard_map/ppermute | solution.py:34
  215.5 54.4 %collective-permute-start.31 = (bf16[384,1536]{1,0:T(8,128)(2,1)}, bf16[384,1536]{1,0:T(8,128)(2,1)S(1)}, u32[]{:S(2)}, u32[]{:S(2)}) collective-permute-start(bf16[384,1536]{1,0:T(8,128)(2,1)} %slice.125), channel_id=1, source_target_pairs={{0,1},{1,0},{2,3},{3,2},{4,5},{5,4},{6,7},{7,6},{8,9},{9,8},{10,11... | collective-permute-start | bytes 3538952 | tf_op jit(solution)/shard_map/ppermute | solution.py:34
  238.2 29.6 %collective-permute-start.32 = (bf16[768,384]{1,0:T(8,128)(2,1)S(1)}, bf16[768,384]{1,0:T(8,128)(2,1)S(1)}, u32[]{:S(2)}, u32[]{:S(2)}) collective-permute-start(bf16[768,384]{1,0:T(8,128)(2,1)S(1)} %fusion.7), channel_id=1, source_target_pairs={{0,4},{4,0},{8,12},{12,8},{16,20},{20,16},{24,28},{28,24},{1,5},{5... | collective-permute-start | bytes 1769480 | tf_op jit(solution)/shard_map/ppermute | solution.py:39
  277.6 29.1 %collective-permute-start.34 = (bf16[384,1536]{1,0:T(8,128)(2,1)}, bf16[384,1536]{1,0:T(8,128)(2,1)}, u32[]{:S(2)}, u32[]{:S(2)}) collective-permute-start(bf16[384,1536]{1,0:T(8,128)(2,1)} %pad_maximum_fusion.2), channel_id=1, source_target_pairs={{0,1},{1,0},{2,3},{3,2},{4,5},{5,4},{6,7},{7,6},{8,9},{9,8},{10,11... | collective-permute-start | bytes 3538952 | tf_op jit(solution)/shard_map/ppermute | solution.py:34
  298.1 53.9 %collective-permute-start.40 = (bf16[1536,384]{1,0:T(8,128)(2,1)}, bf16[1536,384]{1,0:T(8,128)(2,1)}, u32[]{:S(2)}, u32[]{:S(2)}) collective-permute-start(bf16[1536,384]{1,0:T(8,128)(2,1)} %fusion.36), channel_id=1, source_target_pairs={{0,1},{1,0},{2,3},{3,2},{4,5},{5,4},{6,7},{7,6},{8,9},{9,8},{10,11... | collective-permute-start | bytes 3538952 | tf_op jit(solution)/shard_map/ppermute | solution.py:34
  299.1 31.6 %collective-permute-start.38 = (bf16[768,384]{1,0:T(8,128)(2,1)S(1)}, bf16[768,384]{1,0:T(8,128)(2,1)}, u32[]{:S(2)}, u32[]{:S(2)}) collective-permute-start(bf16[768,384]{1,0:T(8,128)(2,1)S(1)} %add_convert_fusion.10), channel_id=1, source_target_pairs={{0,16},{4,20},{8,24},{12,28},{16,0},{20,4},{24,8},{28,12},{1,17},{... | collective-permute-start | bytes 1769480 | tf_op jit(solution)/shard_map/ppermute | solution.py:39
  304.2 29.1 %collective-permute-start.37 = (bf16[192,1536]{1,0:T(8,128)(2,1)S(1)}, bf16[192,1536]{1,0:T(8,128)(2,1)}, u32[]{:S(2)}, u32[]{:S(2)}) collective-permute-start(bf16[192,1536]{1,0:T(8,128)(2,1)S(1)} %fusion.3), channel_id=1, source_target_pairs={{0,8},{4,12},{8,0},{12,4},{16,24},{20,28},{24,16},{28,20},{1,9},{5... | collective-permute-start | bytes 1769480 | tf_op jit(solution)/shard_map/ppermute | solution.py:39
  308.8 38.7 %collective-permute-start.41 = (bf16[192,1536]{1,0:T(8,128)(2,1)}, bf16[192,1536]{1,0:T(8,128)(2,1)}, u32[]{:S(2)}, u32[]{:S(2)}) collective-permute-start(bf16[192,1536]{1,0:T(8,128)(2,1)} %fusion.9), channel_id=1, source_target_pairs={{0,4},{4,0},{8,12},{12,8},{16,20},{20,16},{24,28},{28,24},{1,5},{5... | collective-permute-start | bytes 1769480 | tf_op jit(solution)/shard_map/ppermute | solution.py:39
  330.7 58.2 %collective-permute-start.42 = (bf16[384,1536]{1,0:T(8,128)(2,1)}, bf16[384,1536]{1,0:T(8,128)(2,1)}, u32[]{:S(2)}, u32[]{:S(2)}) collective-permute-start(bf16[384,1536]{1,0:T(8,128)(2,1)} %slice.127), channel_id=1, source_target_pairs={{0,1},{1,0},{2,3},{3,2},{4,5},{5,4},{6,7},{7,6},{8,9},{9,8},{10,11... | collective-permute-start | bytes 3538952 | tf_op jit(solution)/shard_map/ppermute | solution.py:34
  333.3 44.0 %collective-permute-start.46 = (bf16[768,384]{1,0:T(8,128)(2,1)S(1)}, bf16[768,384]{1,0:T(8,128)(2,1)S(1)}, u32[]{:S(2)}, u32[]{:S(2)}) collective-permute-start(bf16[768,384]{1,0:T(8,128)(2,1)S(1)} %add_convert_fusion.8.refs_2_), channel_id=1, source_target_pairs={{0,4},{4,0},{8,12},{12,8},{16,20},{20,16},{24,28},{28,24},{1,5},{5... | collective-permute-start | bytes 1769480 | tf_op jit(solution)/shard_map/ppermute | solution.py:39
  336.3 42.0 %collective-permute-start.45 = (bf16[192,1536]{1,0:T(8,128)(2,1)S(1)}, bf16[192,1536]{1,0:T(8,128)(2,1)S(1)}, u32[]{:S(2)}, u32[]{:S(2)}) collective-permute-start(bf16[192,1536]{1,0:T(8,128)(2,1)S(1)} %add_convert_fusion.7), channel_id=1, source_target_pairs={{0,16},{4,20},{8,24},{12,28},{16,0},{20,4},{24,8},{28,12},{1,17},{... | collective-permute-start | bytes 1769480 | tf_op jit(solution)/shard_map/ppermute | solution.py:39
  349.9 33.8 %collective-permute-start.44 = (bf16[192,1536]{1,0:T(8,128)(2,1)}, bf16[192,1536]{1,0:T(8,128)(2,1)}, u32[]{:S(2)}, u32[]{:S(2)}) collective-permute-start(bf16[192,1536]{1,0:T(8,128)(2,1)} %fusion.2), channel_id=1, source_target_pairs={{0,8},{4,12},{8,0},{12,4},{16,24},{20,28},{24,16},{28,20},{1,9},{5... | collective-permute-start | bytes 1769480 | tf_op jit(solution)/shard_map/ppermute | solution.py:39
  354.1 31.9 %collective-permute-start.43 = (bf16[768,384]{1,0:T(8,128)(2,1)}, bf16[768,384]{1,0:T(8,128)(2,1)}, u32[]{:S(2)}, u32[]{:S(2)}) collective-permute-start(bf16[768,384]{1,0:T(8,128)(2,1)} %fusion.10), channel_id=1, source_target_pairs={{0,4},{4,0},{8,12},{12,8},{16,20},{20,16},{24,28},{28,24},{1,5},{5... | collective-permute-start | bytes 1769480 | tf_op jit(solution)/shard_map/ppermute | solution.py:39
  378.2 38.7 %collective-permute-start.50 = (bf16[384,1152]{1,0:T(8,128)(2,1)}, bf16[384,1152]{1,0:T(8,128)(2,1)}, u32[]{:S(2)}, u32[]{:S(2)}) collective-permute-start(bf16[384,1152]{1,0:T(8,128)(2,1)} %pad_maximum_fusion.3), channel_id=1, source_target_pairs={{0,1},{1,0},{2,3},{3,2},{4,5},{5,4},{6,7},{7,6},{8,9},{9,8},{10,11... | collective-permute-start | bytes 2654216 | tf_op jit(solution)/shard_map/ppermute | solution.py:34
  380.6 31.3 %collective-permute-start.51 = (bf16[192,1536]{1,0:T(8,128)(2,1)S(1)}, bf16[192,1536]{1,0:T(8,128)(2,1)S(1)}, u32[]{:S(2)}, u32[]{:S(2)}) collective-permute-start(bf16[192,1536]{1,0:T(8,128)(2,1)S(1)} %add_convert_fusion.5.refs_2_), channel_id=1, source_target_pairs={{0,4},{4,0},{8,12},{12,8},{16,20},{20,16},{24,28},{28,24},{1,5},{5... | collective-permute-start | bytes 1769480 | tf_op jit(solution)/shard_map/ppermute | solution.py:39
  388.4 33.2 %collective-permute-start.49 = (bf16[768,384]{1,0:T(8,128)(2,1)}, bf16[768,384]{1,0:T(8,128)(2,1)}, u32[]{:S(2)}, u32[]{:S(2)}) collective-permute-start(bf16[768,384]{1,0:T(8,128)(2,1)} %fusion.1), channel_id=1, source_target_pairs={{0,8},{4,12},{8,0},{12,4},{16,24},{20,28},{24,16},{28,20},{1,9},{5... | collective-permute-start | bytes 1769480 | tf_op jit(solution)/shard_map/ppermute | solution.py:39
  391.5 32.6 %collective-permute-start.48 = (bf16[192,1536]{1,0:T(8,128)(2,1)}, bf16[192,1536]{1,0:T(8,128)(2,1)}, u32[]{:S(2)}, u32[]{:S(2)}) collective-permute-start(bf16[192,1536]{1,0:T(8,128)(2,1)} %get-tuple-element.421), channel_id=1, source_target_pairs={{0,4},{4,0},{8,12},{12,8},{16,20},{20,16},{24,28},{28,24},{1,5},{5... | collective-permute-start | bytes 1769480 | tf_op jit(solution)/shard_map/ppermute | solution.py:39
  392.9 37.3 %collective-permute-start.53 = (bf16[192,1536]{1,0:T(8,128)(2,1)}, bf16[192,1536]{1,0:T(8,128)(2,1)}, u32[]{:S(2)}, u32[]{:S(2)}) collective-permute-start(bf16[192,1536]{1,0:T(8,128)(2,1)} %add_convert_fusion.4), channel_id=1, source_target_pairs={{0,16},{4,20},{8,24},{12,28},{16,0},{20,4},{24,8},{28,12},{1,17},{... | collective-permute-start | bytes 1769480 | tf_op jit(solution)/shard_map/ppermute | solution.py:39
  412.8 20.7 %collective-permute-start.55 = (bf16[384,384]{1,0:T(8,128)(2,1)}, bf16[384,384]{1,0:T(8,128)(2,1)}, u32[]{:S(2)}, u32[]{:S(2)}) collective-permute-start(bf16[384,384]{1,0:T(8,128)(2,1)} %fusion.43), channel_id=1, source_target_pairs={{0,1},{1,0},{2,3},{3,2},{4,5},{5,4},{6,7},{7,6},{8,9},{9,8},{10,11... | collective-permute-start | bytes 884744 | tf_op jit(solution)/shard_map/ppermute | solution.py:34
  421.6 49.9 %collective-permute-start.59 = (f32[80,384]{1,0:T(8,128)}, f32[80,384]{1,0:T(8,128)}, u32[]{:S(2)}, u32[]{:S(2)}) collective-permute-start(f32[80,384]{1,0:T(8,128)} %get-tuple-element.373), channel_id=1, source_target_pairs={{0,1},{1,0},{2,3},{3,2},{4,5},{5,4},{6,7},{7,6},{8,9},{9,8},{10,11... | collective-permute-start | bytes 368648 | tf_op jit(solution)/shard_map/ppermute | solution.py:34
  430.1 94.2 %all-gather.7.cloned.1.call-start = ((), (), s32[]{:S(2)}) async-start(), calls=%async_computation.1 | async-start | bytes 2359296 | tf_op jit(solution)/shard_map/all_gather | solution.py:703
  430.2 36.3 %collective-permute-start.63 = (bf16[768,384]{1,0:T(8,128)(2,1)}, bf16[768,384]{1,0:T(8,128)(2,1)S(1)}, u32[]{:S(2)}, u32[]{:S(2)}) collective-permute-start(bf16[768,384]{1,0:T(8,128)(2,1)} %add_convert_fusion.2), channel_id=1, source_target_pairs={{0,16},{4,20},{8,24},{12,28},{16,0},{20,4},{24,8},{28,12},{1,17},{... | collective-permute-start | bytes 1769480 | tf_op jit(solution)/shard_map/ppermute | solution.py:39
  436.8 34.3 %collective-permute-start.52 = (f32[1024,384]{1,0:T(8,128)S(1)}, f32[1024,384]{1,0:T(8,128)S(1)}, u32[]{:S(2)}, u32[]{:S(2)}) collective-permute-start(f32[1024,384]{1,0:T(8,128)S(1)} %copy-done.117), channel_id=1, source_target_pairs={{0,2},{2,0},{1,3},{3,1},{4,6},{6,4},{5,7},{7,5},{8,10},{10,8},{9,1... | collective-permute-start | bytes 4718600 | tf_op jit(solution)/shard_map/ppermute | solution.py:34
  497.3 29.9 %collective-permute-start.74 = (bf16[192,1536]{1,0:T(8,128)(2,1)S(1)}, bf16[192,1536]{1,0:T(8,128)(2,1)}, u32[]{:S(2)}, u32[]{:S(2)}) collective-permute-start(bf16[192,1536]{1,0:T(8,128)(2,1)S(1)} %maximum_select_fusion.refs_0_), channel_id=1, source_target_pairs={{0,4},{4,0},{8,12},{12,8},{16,20},{20,16},{24,28},{28,24},{1,5},{5... | collective-permute-start | bytes 1769480 | tf_op jit(solution)/shard_map/ppermute | solution.py:39
  499.1 32.0 %collective-permute-start.73 = (bf16[192,384]{1,0:T(8,128)(2,1)}, bf16[192,384]{1,0:T(8,128)(2,1)}, u32[]{:S(2)}, u32[]{:S(2)}) collective-permute-start(bf16[192,384]{1,0:T(8,128)(2,1)} %add_convert_fusion.18.refs_2_), channel_id=1, source_target_pairs={{0,4},{4,0},{8,12},{12,8},{16,20},{20,16},{24,28},{28,24},{1,5},{5... | collective-permute-start | bytes 442376 | tf_op jit(solution)/shard_map/ppermute | solution.py:39
  499.4 31.7 %collective-permute-start.72 = (bf16[192,1152]{1,0:T(8,128)(2,1)S(1)}, bf16[192,1152]{1,0:T(8,128)(2,1)}, u32[]{:S(2)}, u32[]{:S(2)}) collective-permute-start(bf16[192,1152]{1,0:T(8,128)(2,1)S(1)} %maximum_select_fusion.1.refs_0_), channel_id=1, source_target_pairs={{0,4},{4,0},{8,12},{12,8},{16,20},{20,16},{24,28},{28,24},{1,5},{5... | collective-permute-start | bytes 1327112 | tf_op jit(solution)/shard_map/ppermute | solution.py:39
  (189 other events, 1588.7 us)
Sparse Core Ops, SparseCore 0:
  430.2 27.3 all-gather.4
  497.3 26.8 all-gather.6
where the time goes:
time: 549 us; the launch traced here: 542 us
  Pallas kernels  184 us (34%)
  starting transfers between devices  87.9 us (16%)
  waiting for transfers between devices  86.6 us (16%)
  other arithmetic  66.4 us (12%)
  local copies, waits for them, and re-layouts  63.5 us (12%)
  matrix products  37.6 us (7%)
  between operations  16.6 us (3%)
    pallas_call x14, Pallas kernels, token_kernel(): pl.pallas_call(kernel, grid=(length // block,), in_specs=in_specs, out_sp...  93.7 us
    ppermute x39, starting transfers between devices, swap_bit(): return lax.ppermute(value, DP, [(i, i ^ 1 << bit) for i in range(count)])  57.8 us
    ppermute x39, waiting for transfers between devices, swap_bit(): return lax.ppermute(value, DP, [(i, i ^ 1 << bit) for i in range(count)])  51.6 us
    pallas_call x3, Pallas kernels, attend_backward(): pl.pallas_call(partial(backward_kernel, scale=scale, start=start), grid_s...  51.2 us
    dot_general x16, matrix products, dot_tn(): lax.dot_general(left, right, (((0,), (0,)), ((), ())), preferred_element_...  37.6 us
    convert_element_type x26, other arithmetic, step(): self.sent = sum((part.astype(F32) for part in parts)).astype(BF16)  31.5 us
    unnamed x293, local copies, waits for them, and re-layouts  30.6 us
    pallas_call x2, Pallas kernels, attend_forward(): pl.pallas_call(partial(forward_kernel, scale=scale), grid_spec=pltpu.Pref...  24.9 us
  transfers between devices with their start and end apart: 77, of which 22 were waited for; matrix products, arithmetic and copies ran while one was open for 26% of the time, Pallas kernels for 27%

commit v1 on v0

--- a/solution.py
+++ b/solution.py
@@ -12,7 +12,7 @@
 EPSILON = 1e-06
 MASKED_SCORE = -1e30
 LANES = 128
-SMALL_SLOTS = 8
+SMALL_SLOTS = (8, 9)
 TOKEN_BLOCK = 512
 LAYERS = 2
 QKV, OUT, UP, DOWN = range(4)
@@ -227,14 +227,17 @@
 
 
 def middle_blocks(blocks, slots, most, work):
-    small = min(SMALL_SLOTS, slots)
-
-    @pl.when(most <= small)
-    def _():
-        for block in range(1, blocks - 1):
-            work(block, small)
-
-    @pl.when(most > small)
+    low = 0
+    for size in SMALL_SLOTS:
+
+        @pl.when((most > low) & (most <= size))
+        def _():
+            for block in range(1, blocks - 1):
+                work(block, min(size, slots))
+
+        low = size
+
+    @pl.when(most > low)
     def _():
         def body(block, carry):
             work(block, slots)
@@ -906,8 +909,6 @@
         w[OUT] = weight(layer, OUT)
         part = kernel(product_kernel, [mixed], [w[OUT]], halves_out)
         got = swap_row(part)
-        if layer == layers - 1:
-            goal.pass_on(line)
         if layer == 0:
             ask(1, UP, 0)
             ask(1, DOWN, None)
@@ -920,6 +921,8 @@
             halves_out + [(width, F32), (width, BF16), (width, BF16), (1, F32), (feed, BF16), (feed, BF16)],
         )
         got = swap_row(part)
+        if layer == layers - 1:
+            goal.pass_on(line)
         if layer == 0:
             if layers > 1:
                 shard[1] = line.mark(line.next(qkv_weight[1]).reshape(half, 3 * inner))

time: 549 us -> 548 us (level)
  transfers between devices with their start and end apart: 77 -> 77, of which waited for: 22 -> 26; matrix products, arithmetic and copies ran while one was open for 26% -> 26% of each run, Pallas kernels for 27% -> 27%
where the time goes in v1:
time: 548 us; the launch traced here: 541 us
  Pallas kernels  184 us (34%)
  starting transfers between devices  88.4 us (16%)
  waiting for transfers between devices  85.2 us (16%)
  other arithmetic  66.3 us (12%)
  local copies, waits for them, and re-layouts  63.5 us (12%)
  matrix products  37.6 us (7%)
  between operations  16.5 us (3%)
    pallas_call x14, Pallas kernels, token_kernel(): pl.pallas_call(kernel, grid=(length // block,), in_specs=in_specs, out_sp...  92.5 us
    ppermute x39, starting transfers between devices, swap_bit(): return lax.ppermute(value, DP, [(i, i ^ 1 << bit) for i in range(count)])  56.1 us
    ppermute x39, waiting for transfers between devices, swap_bit(): return lax.ppermute(value, DP, [(i, i ^ 1 << bit) for i in range(count)])  54.9 us
    pallas_call x3, Pallas kernels, attend_backward(): pl.pallas_call(partial(backward_kernel, scale=scale, start=start), grid_s...  51.9 us
    dot_general x16, matrix products, dot_tn(): lax.dot_general(left, right, (((0,), (0,)), ((), ())), preferred_element_...  37.6 us
    convert_element_type x26, other arithmetic, step(): self.sent = sum((part.astype(F32) for part in parts)).astype(BF16)  31.4 us
    unnamed x293, local copies, waits for them, and re-layouts  30.6 us
    pallas_call x2, Pallas kernels, attend_forward(): pl.pallas_call(partial(forward_kernel, scale=scale), grid_spec=pltpu.Pref...  25.2 us
  transfers between devices with their start and end apart: 77, of which 26 were waited for; matrix products, arithmetic and copies ran while one was open for 26% of the time, Pallas kernels for 27%

profile of v1, /device:TPU:0, one launch (start us, length us, event | category | flops | bytes accessed | tf_op | source)
XLA Modules:
  0.0 541.3 jit_solution(8727926224510520319)
XLA Ops:
  33.4 4.9 collective-permute-start.5
  42.0 6.9 %collective-permute-done.4.refs_6_.refs_5_ = bf16[192,1152]{1,0:T(8,128)(2,1)S(1)} collective-permute-done((bf16[192,1152]{1,0:T(8,128)(2,1)S(1)}, bf16[192,1152]{1,0:T(8,128)(2,1)S(1)}, u32[]{:S(2)}, u32[]{:S(2)}) %collective-permute-start.4) | collective-permute-done | bytes 442400 | tf_op jit(solution)/shard_map/ppermute | solution.py:39
  69.5 12.5 %shard_map.298 = (bf16[1024,384]{1,0:T(8,128)(2,1)S(1)}, f32[3,16,128]{2,1,0:T(8,128)S(1)}) custom-call(s32[3,14,11]{2,1,0:T(8,128)S(1)} %bitcast.165, s32[3]{0:T(128)S(1)} %get-tuple-element.442.most_ref, bf16[1024,1152]{1,0:T(8,128)(2,1)S(1)} %shard_map.297.q_ref.k_ref.v_ref, bf16[1024,1152]{1,0:T(8,128)(2,1)S(1)} %shard_map.297.q_ref.k_ref.v_ref, ...), custom_call_target="tpu_custom_call" | custom-call | tf_op jit(solution)/shard_map/pallas_call | solution.py:361
  94.1 5.9 %collective-permute-done.13.refs_10_.refs_4_ = bf16[192,1152]{1,0:T(8,128)(2,1)S(1)} collective-permute-done((bf16[192,1152]{1,0:T(8,128)(2,1)S(1)}, bf16[192,1152]{1,0:T(8,128)(2,1)S(1)}, u32[]{:S(2)}, u32[]{:S(2)}) %collective-permute-start.13) | collective-permute-done | bytes 442400 | tf_op jit(solution)/shard_map/ppermute | solution.py:39
  102.6 13.7 %shard_map.300 = (bf16[1024,384]{1,0:T(8,128)(2,1)}, bf16[1024,384]{1,0:T(8,128)(2,1)}, f32[1024,768]{1,0:T(8,128)}, bf16[1024,768]{1,0:T(8,128)(2,1)}, bf16[102...) custom-call(s32[1,1]{1,0:T(1,128)} %bitcast.refs_0_.place_ref, ...), custom_call_target="tpu_custom_call" | custom-call | tf_op jit(solution)/shard_map/pallas_call | solution.py:483
  126.2 7.3 %shard_map.301 = (f32[1024,768]{1,0:T(8,128)}, bf16[1024,384]{1,0:T(8,128)(2,1)S(1)}, bf16[1024,384]{1,0:T(8,128)(2,1)S(1)}, bf16[1024,768]{1,0:T(8,128)(2,1)}, ...) custom-call(s32[1,1]{1,0:T(1,128)} %bitcast.refs_0_.place_ref, bf16[1024,384]{1,0:T(8,128)(2,1)} %get-tuple-element.246.refs_1_, ...), custom_call_target="tpu_custom_call" | custom-call | tf_op jit(solution)/shard_map/pallas_call | solution.py:483
  138.6 12.7 %shard_map.302 = (bf16[1024,384]{1,0:T(8,128)(2,1)S(1)}, f32[3,16,128]{2,1,0:T(8,128)S(1)}) custom-call(s32[3,14,11]{2,1,0:T(8,128)S(1)} %bitcast.168, s32[3]{0:T(128)S(1)} %copy-done.96, bf16[1024,1152]{1,0:T(8,128)(2,1)S(1)} %copy-done.2, bf16[1024,1152]{1,0:T(8,128)(2,1)S(1)} %copy-done.2, bf16[1024,1152]{1,0:T(8,128)(2,1)S(1)} %copy-done.2, ...), custom_call_target="tpu_custom_call" | custom-call | tf_op jit(solution)/shard_map/pallas_call | solution.py:361
  151.4 7.0 %collective-permute-done.20.refs_12_.refs_5_ = bf16[1536,384]{1,0:T(8,128)(2,1)} collective-permute-done((bf16[1536,384]{1,0:T(8,128)(2,1)}, bf16[1536,384]{1,0:T(8,128)(2,1)}, u32[]{:S(2)}, u32[]{:S(2)}) %collective-permute-start.20) | collective-permute-done | bytes 1179680 | tf_op jit(solution)/shard_map/ppermute | solution.py:34
  164.9 14.0 %shard_map.304 = (bf16[1024,384]{1,0:T(8,128)(2,1)S(1)}, bf16[1024,384]{1,0:T(8,128)(2,1)S(1)}, f32[1024,768]{1,0:T(8,128)}, bf16[1024,768]{1,0:T(8,128)(2,1)}, ...) custom-call(s32[1,1]{1,0:T(1,128)} %bitcast.refs_0_.place_ref, ...), custom_call_target="tpu_custom_call" | custom-call | tf_op jit(solution)/shard_map/pallas_call | solution.py:483
  186.8 7.3 %shard_map.305 = (f32[1024,768]{1,0:T(8,128)}, f32[1024,384]{1,0:T(8,128)}, bf16[1024,384]{1,0:T(8,128)(2,1)S(1)}, bf16[1024,384]{1,0:T(8,128)(2,1)S(1)}, bf16[1...) custom-call(s32[1,1]{1,0:T(1,128)} %bitcast.refs_0_.place_ref, ...), custom_call_target="tpu_custom_call" | custom-call | tf_op jit(solution)/shard_map/pallas_call | solution.py:483
  197.0 9.5 %shard_map.306 = (bf16[1024,768]{1,0:T(8,128)(2,1)}, bf16[1024,1536]{1,0:T(8,128)(2,1)}, f32[8,384]{1,0:T(8,128)S(1)}) custom-call(s32[1,1]{1,0:T(1,128)} %bitcast.refs_0_.place_ref, bf16[1024,384]{1,0:T(8,128)(2,1)S(1)} %get-tuple-element.280.refs_1_, bf16[1024,384]{1,0:T(8,128)(2,1)S(1)} %get-tuple-element.272.refs_2_, ...), custom_call_target="tpu_custom_call" | custom-call | tf_op jit(solution)/shard_map/pallas_call | solution.py:483
  208.3 5.0 fusion.30
  218.6 5.9 %shard_map.307 = (f32[1024,384]{1,0:T(8,128)S(1)}, f32[1024,384]{1,0:T(8,128)}, bf16[1024,384]{1,0:T(8,128)(2,1)S(1)}, bf16[1024,384]{1,0:T(8,128)(2,1)S(1)}, bf...) custom-call(s32[1,1]{1,0:T(1,128)} %bitcast.refs_0_.place_ref, bf16[1024,768]{1,0:T(8,128)(2,1)} %get-tuple-element.281.refs_1_, ...), custom_call_target="tpu_custom_call" | custom-call | tf_op jit(solution)/shard_map/pallas_call | solution.py:483
  227.3 8.8 %collective-permute-done.30 = bf16[1536,384]{1,0:T(8,128)(2,1)} collective-permute-done((bf16[1536,384]{1,0:T(8,128)(2,1)}, bf16[1536,384]{1,0:T(8,128)(2,1)}, u32[]{:S(2)}, u32[]{:S(2)}) %collective-permute-start.30) | collective-permute-done | bytes 1179680 | tf_op jit(solution)/shard_map/ppermute | solution.py:34
  239.0 25.7 %shard_map.308.refs_1_ = bf16[1024,1152]{1,0:T(8,128)(2,1)S(1)} custom-call(s32[3,14,11]{2,1,0:T(8,128)S(1)} %bitcast.169, s32[3]{0:T(128)S(1)} %copy-done.97, bf16[1024,1152]{1,0:T(8,128)(2,1)} %get-tuple-element.251.q_ref.k_ref.v_ref, bf16[1024,1152]{1,0:T(8,128)(2,1)} %get-tuple-element.251.q_ref.k_ref.v_ref, ...), custom_call_target="tpu_custom_call" | custom-call | tf_op jit(solution)/shard_map/pallas_call | solution.py:387
  271.2 3.9 shard_map.309
  286.3 5.7 %shard_map.310 = (f32[1024,768]{1,0:T(8,128)}, bf16[1024,384]{1,0:T(8,128)(2,1)S(1)}, bf16[1024,384]{1,0:T(8,128)(2,1)S(1)}, f32[8,768]{1,0:T(8,128)S(1)}) custom-call(s32[1,1]{1,0:T(1,128)} %bitcast.refs_0_.place_ref, bf16[1024,768]{1,0:T(8,128)(2,1)} %get-tuple-element.301.refs_1_, bf16[1024,768]{1,0:T(8,128)(2,1)} %collective-permute-done.33.refs_2_, ...), custom_call_target="tpu_custom_call" | custom-call | tf_op jit(solution)/shard_map/pallas_call | solution.py:483
  292.0 5.0 fusion.36
  297.8 5.1 collective-permute-start.38
  307.9 9.1 %shard_map.311 = (bf16[1024,768]{1,0:T(8,128)(2,1)S(1)}, bf16[1024,1536]{1,0:T(8,128)(2,1)}, f32[8,384]{1,0:T(8,128)S(1)}) custom-call(s32[1,1]{1,0:T(1,128)} %bitcast.refs_0_.place_ref, bf16[1024,384]{1,0:T(8,128)(2,1)S(1)} %get-tuple-element.320.refs_1_, bf16[1024,384]{1,0:T(8,128)(2,1)S(1)} %get-tuple-element.309.refs_2_, ...), custom_call_target="tpu_custom_call" | custom-call | tf_op jit(solution)/shard_map/pallas_call | solution.py:483
  317.1 5.1 fusion.37
  337.6 6.5 %shard_map.312 = (f32[1024,384]{1,0:T(8,128)S(1)}, f32[1024,384]{1,0:T(8,128)}, bf16[1024,384]{1,0:T(8,128)(2,1)S(1)}, bf16[1024,384]{1,0:T(8,128)(2,1)S(1)}, bf...) custom-call(s32[1,1]{1,0:T(1,128)} %bitcast.refs_0_.place_ref, bf16[1024,768]{1,0:T(8,128)(2,1)} %copy-done.40, ...), custom_call_target="tpu_custom_call" | custom-call | tf_op jit(solution)/shard_map/pallas_call | solution.py:483
  354.9 17.3 %shard_map.313.refs_1_ = bf16[1024,768]{1,0:T(8,128)(2,1)S(1)} custom-call(s32[3,14,11]{2,1,0:T(8,128)S(1)} %bitcast.166, s32[3]{0:T(128)S(1)} %get-tuple-element.442.most_ref, bf16[1024,1152]{1,0:T(8,128)(2,1)S(1)} %shard_map.297.q_ref.k_ref.v_ref, bf16[1024,1152]{1,0:T(8,128)(2,1)S(1)} %shard_map.297.q_ref.k_ref.v_ref, ...), custom_call_target="tpu_custom_call" | custom-call | tf_op jit(solution)/shard_map/pallas_call | solution.py:387
  393.8 8.8 %shard_map.314.refs_2_ = bf16[1024,384]{1,0:T(8,128)(2,1)S(1)} custom-call(s32[3,14,11]{2,1,0:T(8,128)S(1)} %bitcast.167, s32[3]{0:T(128)S(1)} %get-tuple-element.442.most_ref, bf16[1024,1152]{1,0:T(8,128)(2,1)S(1)} %shard_map.297.q_ref.k_ref.v_ref, bf16[1024,1152]{1,0:T(8,128)(2,1)S(1)} %shard_map.297.q_ref.k_ref.v_ref, ...), custom_call_target="tpu_custom_call" | custom-call | tf_op jit(solution)/shard_map/pallas_call | solution.py:387
  441.5 10.7 %collective-permute-done.58 = bf16[96,1152]{1,0:T(8,128)(2,1)S(1)} collective-permute-done((bf16[96,1152]{1,0:T(8,128)(2,1)S(1)}, bf16[96,1152]{1,0:T(8,128)(2,1)S(1)}, u32[]{:S(2)}, u32[]{:S(2)}) %collective-permute-start.58) | collective-permute-done | bytes 221216 | tf_op jit(solution)/shard_map/ppermute | solution.py:39
  457.2 9.4 %collective-permute-done.63 = bf16[768,384]{1,0:T(8,128)(2,1)S(1)} collective-permute-done((bf16[768,384]{1,0:T(8,128)(2,1)}, bf16[768,384]{1,0:T(8,128)(2,1)S(1)}, u32[]{:S(2)}, u32[]{:S(2)}) %collective-permute-start.63) | collective-permute-done | bytes 589856 | tf_op jit(solution)/shard_map/ppermute | solution.py:39
  475.5 4.9 collective-permute-done.65.refs_1_
  485.8 4.2 collective-permute-done.70
  490.9 3.9 collective-permute-done.68
  500.5 4.0 collective-permute-done.71
  526.0 3.9 shard_map.319
  529.9 4.3 shard_map.320
  (586 shorter events, 265.8 us)
Async XLA Ops:
  7.2 507.3 %all-gather.5.cloned.1.call-start = ((), (), s32[]{:S(2)}) async-start(), calls=%async_computation | async-start | bytes 2359296 | tf_op jit(solution)/shard_map/all_gather | solution.py:706
  39.9 21.9 %collective-permute-start.6 = (bf16[192,1536]{1,0:T(8,128)(2,1)}, bf16[192,1536]{1,0:T(8,128)(2,1)}, u32[]{:S(2)}, u32[]{:S(2)}) collective-permute-start(bf16[192,1536]{1,0:T(8,128)(2,1)} %dynamic-slice_bitcast_fusion.1), channel_id=1, source_target_pairs={{0,1},{1,0},{2,3},{3,2},{4,5},{5,4},{6,7},{7,6},{8,9},{9,8},{10,11... | collective-permute-start | bytes 1769480 | tf_op jit(solution)/shard_map/ppermute | solution.py:34
  61.8 20.8 %collective-permute-start.10 = (bf16[192,1536]{1,0:T(8,128)(2,1)}, bf16[192,1536]{1,0:T(8,128)(2,1)}, u32[]{:S(2)}, u32[]{:S(2)}) collective-permute-start(bf16[192,1536]{1,0:T(8,128)(2,1)} %collective-permute-done.6.refs_10_.refs_8_), channel_id=1, source_target_pairs={{0,4},{4,0},{8,12},{12,8},{16,20},{20,16},{24,28},{28,24},{1,5},{5... | collective-permute-start | bytes 1769480 | tf_op jit(solution)/shard_map/ppermute | solution.py:39
  65.0 21.1 %collective-permute-start.16 = (f32[6,2,384]{2,0,1:T(8,128)}, f32[6,2,384]{2,0,1:T(8,128)}, u32[]{:S(2)}, u32[]{:S(2)}) collective-permute-start(f32[6,2,384]{2,0,1:T(8,128)} %stack.34), channel_id=1, source_target_pairs={{0,1},{1,0},{2,3},{3,2},{4,5},{5,4},{6,7},{7,6},{8,9},{9,8},{10,11... | collective-permute-start | bytes 55304 | tf_op jit(solution)/shard_map/ppermute | solution.py:34
  119.3 39.1 %collective-permute-start.20 = (bf16[1536,384]{1,0:T(8,128)(2,1)}, bf16[1536,384]{1,0:T(8,128)(2,1)}, u32[]{:S(2)}, u32[]{:S(2)}) collective-permute-start(bf16[1536,384]{1,0:T(8,128)(2,1)} %slice_bitcast_fusion), channel_id=1, source_target_pairs={{0,1},{1,0},{2,3},{3,2},{4,5},{5,4},{6,7},{7,6},{8,9},{9,8},{10,11... | collective-permute-start | bytes 3538952 | tf_op jit(solution)/shard_map/ppermute | solution.py:34
  206.9 29.1 %collective-permute-start.30 = (bf16[1536,384]{1,0:T(8,128)(2,1)}, bf16[1536,384]{1,0:T(8,128)(2,1)}, u32[]{:S(2)}, u32[]{:S(2)}) collective-permute-start(bf16[1536,384]{1,0:T(8,128)(2,1)} %fusion.29), channel_id=1, source_target_pairs={{0,1},{1,0},{2,3},{3,2},{4,5},{5,4},{6,7},{7,6},{8,9},{9,8},{10,11... | collective-permute-start | bytes 3538952 | tf_op jit(solution)/shard_map/ppermute | solution.py:34
  214.5 54.7 %collective-permute-start.31 = (bf16[384,1536]{1,0:T(8,128)(2,1)}, bf16[384,1536]{1,0:T(8,128)(2,1)S(1)}, u32[]{:S(2)}, u32[]{:S(2)}) collective-permute-start(bf16[384,1536]{1,0:T(8,128)(2,1)} %slice.125), channel_id=1, source_target_pairs={{0,1},{1,0},{2,3},{3,2},{4,5},{5,4},{6,7},{7,6},{8,9},{9,8},{10,11... | collective-permute-start | bytes 3538952 | tf_op jit(solution)/shard_map/ppermute | solution.py:34
  237.3 29.8 %collective-permute-start.32 = (bf16[768,384]{1,0:T(8,128)(2,1)S(1)}, bf16[768,384]{1,0:T(8,128)(2,1)S(1)}, u32[]{:S(2)}, u32[]{:S(2)}) collective-permute-start(bf16[768,384]{1,0:T(8,128)(2,1)S(1)} %fusion.7), channel_id=1, source_target_pairs={{0,4},{4,0},{8,12},{12,8},{16,20},{20,16},{24,28},{28,24},{1,5},{5... | collective-permute-start | bytes 1769480 | tf_op jit(solution)/shard_map/ppermute | solution.py:39
  276.4 29.1 %collective-permute-start.34 = (bf16[384,1536]{1,0:T(8,128)(2,1)}, bf16[384,1536]{1,0:T(8,128)(2,1)}, u32[]{:S(2)}, u32[]{:S(2)}) collective-permute-start(bf16[384,1536]{1,0:T(8,128)(2,1)} %pad_maximum_fusion.2), channel_id=1, source_target_pairs={{0,1},{1,0},{2,3},{3,2},{4,5},{5,4},{6,7},{7,6},{8,9},{9,8},{10,11... | collective-permute-start | bytes 3538952 | tf_op jit(solution)/shard_map/ppermute | solution.py:34
  281.5 21.4 %collective-permute-start.35 = (bf16[192,1536]{1,0:T(8,128)(2,1)}, bf16[192,1536]{1,0:T(8,128)(2,1)}, u32[]{:S(2)}, u32[]{:S(2)}) collective-permute-start(bf16[192,1536]{1,0:T(8,128)(2,1)} %fusion.8), channel_id=1, source_target_pairs={{0,4},{4,0},{8,12},{12,8},{16,20},{20,16},{24,28},{28,24},{1,5},{5... | collective-permute-start | bytes 1769480 | tf_op jit(solution)/shard_map/ppermute | solution.py:39
  296.9 54.2 %collective-permute-start.40 = (bf16[1536,384]{1,0:T(8,128)(2,1)}, bf16[1536,384]{1,0:T(8,128)(2,1)}, u32[]{:S(2)}, u32[]{:S(2)}) collective-permute-start(bf16[1536,384]{1,0:T(8,128)(2,1)} %fusion.36), channel_id=1, source_target_pairs={{0,1},{1,0},{2,3},{3,2},{4,5},{5,4},{6,7},{7,6},{8,9},{9,8},{10,11... | collective-permute-start | bytes 3538952 | tf_op jit(solution)/shard_map/ppermute | solution.py:34
  297.8 31.6 %collective-permute-start.38 = (bf16[768,384]{1,0:T(8,128)(2,1)S(1)}, bf16[768,384]{1,0:T(8,128)(2,1)}, u32[]{:S(2)}, u32[]{:S(2)}) collective-permute-start(bf16[768,384]{1,0:T(8,128)(2,1)S(1)} %add_convert_fusion.10), channel_id=1, source_target_pairs={{0,16},{4,20},{8,24},{12,28},{16,0},{20,4},{24,8},{28,12},{1,17},{... | collective-permute-start | bytes 1769480 | tf_op jit(solution)/shard_map/ppermute | solution.py:39
  304.2 27.8 %collective-permute-start.37 = (bf16[192,1536]{1,0:T(8,128)(2,1)S(1)}, bf16[192,1536]{1,0:T(8,128)(2,1)}, u32[]{:S(2)}, u32[]{:S(2)}) collective-permute-start(bf16[192,1536]{1,0:T(8,128)(2,1)S(1)} %fusion.3), channel_id=1, source_target_pairs={{0,8},{4,12},{8,0},{12,4},{16,24},{20,28},{24,16},{28,20},{1,9},{5... | collective-permute-start | bytes 1769480 | tf_op jit(solution)/shard_map/ppermute | solution.py:39
  307.5 38.6 %collective-permute-start.41 = (bf16[192,1536]{1,0:T(8,128)(2,1)}, bf16[192,1536]{1,0:T(8,128)(2,1)}, u32[]{:S(2)}, u32[]{:S(2)}) collective-permute-start(bf16[192,1536]{1,0:T(8,128)(2,1)} %fusion.9), channel_id=1, source_target_pairs={{0,4},{4,0},{8,12},{12,8},{16,20},{20,16},{24,28},{28,24},{1,5},{5... | collective-permute-start | bytes 1769480 | tf_op jit(solution)/shard_map/ppermute | solution.py:39
  329.4 59.4 %collective-permute-start.42 = (bf16[384,1536]{1,0:T(8,128)(2,1)}, bf16[384,1536]{1,0:T(8,128)(2,1)}, u32[]{:S(2)}, u32[]{:S(2)}) collective-permute-start(bf16[384,1536]{1,0:T(8,128)(2,1)} %slice.127), channel_id=1, source_target_pairs={{0,1},{1,0},{2,3},{3,2},{4,5},{5,4},{6,7},{7,6},{8,9},{9,8},{10,11... | collective-permute-start | bytes 3538952 | tf_op jit(solution)/shard_map/ppermute | solution.py:34
  332.0 44.4 %collective-permute-start.46 = (bf16[768,384]{1,0:T(8,128)(2,1)S(1)}, bf16[768,384]{1,0:T(8,128)(2,1)S(1)}, u32[]{:S(2)}, u32[]{:S(2)}) collective-permute-start(bf16[768,384]{1,0:T(8,128)(2,1)S(1)} %add_convert_fusion.8.refs_2_), channel_id=1, source_target_pairs={{0,4},{4,0},{8,12},{12,8},{16,20},{20,16},{24,28},{28,24},{1,5},{5... | collective-permute-start | bytes 1769480 | tf_op jit(solution)/shard_map/ppermute | solution.py:39
  334.9 43.2 %collective-permute-start.45 = (bf16[192,1536]{1,0:T(8,128)(2,1)S(1)}, bf16[192,1536]{1,0:T(8,128)(2,1)S(1)}, u32[]{:S(2)}, u32[]{:S(2)}) collective-permute-start(bf16[192,1536]{1,0:T(8,128)(2,1)S(1)} %add_convert_fusion.7), channel_id=1, source_target_pairs={{0,16},{4,20},{8,24},{12,28},{16,0},{20,4},{24,8},{28,12},{1,17},{... | collective-permute-start | bytes 1769480 | tf_op jit(solution)/shard_map/ppermute | solution.py:39
  348.6 35.5 %collective-permute-start.44 = (bf16[192,1536]{1,0:T(8,128)(2,1)}, bf16[192,1536]{1,0:T(8,128)(2,1)}, u32[]{:S(2)}, u32[]{:S(2)}) collective-permute-start(bf16[192,1536]{1,0:T(8,128)(2,1)} %fusion.2), channel_id=1, source_target_pairs={{0,8},{4,12},{8,0},{12,4},{16,24},{20,28},{24,16},{28,20},{1,9},{5... | collective-permute-start | bytes 1769480 | tf_op jit(solution)/shard_map/ppermute | solution.py:39
  353.1 33.2 %collective-permute-start.43 = (bf16[768,384]{1,0:T(8,128)(2,1)}, bf16[768,384]{1,0:T(8,128)(2,1)}, u32[]{:S(2)}, u32[]{:S(2)}) collective-permute-start(bf16[768,384]{1,0:T(8,128)(2,1)} %fusion.10), channel_id=1, source_target_pairs={{0,4},{4,0},{8,12},{12,8},{16,20},{20,16},{24,28},{28,24},{1,5},{5... | collective-permute-start | bytes 1769480 | tf_op jit(solution)/shard_map/ppermute | solution.py:39
  377.2 38.4 %collective-permute-start.50 = (bf16[384,1152]{1,0:T(8,128)(2,1)}, bf16[384,1152]{1,0:T(8,128)(2,1)}, u32[]{:S(2)}, u32[]{:S(2)}) collective-permute-start(bf16[384,1152]{1,0:T(8,128)(2,1)} %pad_maximum_fusion.3), channel_id=1, source_target_pairs={{0,1},{1,0},{2,3},{3,2},{4,5},{5,4},{6,7},{7,6},{8,9},{9,8},{10,11... | collective-permute-start | bytes 2654216 | tf_op jit(solution)/shard_map/ppermute | solution.py:34
  380.5 31.1 %collective-permute-start.51 = (bf16[192,1536]{1,0:T(8,128)(2,1)S(1)}, bf16[192,1536]{1,0:T(8,128)(2,1)S(1)}, u32[]{:S(2)}, u32[]{:S(2)}) collective-permute-start(bf16[192,1536]{1,0:T(8,128)(2,1)S(1)} %add_convert_fusion.5.refs_2_), channel_id=1, source_target_pairs={{0,4},{4,0},{8,12},{12,8},{16,20},{20,16},{24,28},{28,24},{1,5},{5... | collective-permute-start | bytes 1769480 | tf_op jit(solution)/shard_map/ppermute | solution.py:39
  388.8 31.6 %collective-permute-start.49 = (bf16[768,384]{1,0:T(8,128)(2,1)}, bf16[768,384]{1,0:T(8,128)(2,1)}, u32[]{:S(2)}, u32[]{:S(2)}) collective-permute-start(bf16[768,384]{1,0:T(8,128)(2,1)} %fusion.1), channel_id=1, source_target_pairs={{0,8},{4,12},{8,0},{12,4},{16,24},{20,28},{24,16},{28,20},{1,9},{5... | collective-permute-start | bytes 1769480 | tf_op jit(solution)/shard_map/ppermute | solution.py:39
  391.5 32.2 %collective-permute-start.48 = (bf16[192,1536]{1,0:T(8,128)(2,1)}, bf16[192,1536]{1,0:T(8,128)(2,1)}, u32[]{:S(2)}, u32[]{:S(2)}) collective-permute-start(bf16[192,1536]{1,0:T(8,128)(2,1)} %get-tuple-element.421), channel_id=1, source_target_pairs={{0,4},{4,0},{8,12},{12,8},{16,20},{20,16},{24,28},{28,24},{1,5},{5... | collective-permute-start | bytes 1769480 | tf_op jit(solution)/shard_map/ppermute | solution.py:39
  392.8 37.4 %collective-permute-start.53 = (bf16[192,1536]{1,0:T(8,128)(2,1)}, bf16[192,1536]{1,0:T(8,128)(2,1)}, u32[]{:S(2)}, u32[]{:S(2)}) collective-permute-start(bf16[192,1536]{1,0:T(8,128)(2,1)} %add_convert_fusion.4), channel_id=1, source_target_pairs={{0,16},{4,20},{8,24},{12,28},{16,0},{20,4},{24,8},{28,12},{1,17},{... | collective-permute-start | bytes 1769480 | tf_op jit(solution)/shard_map/ppermute | solution.py:39
  412.4 21.2 %collective-permute-start.55 = (bf16[384,384]{1,0:T(8,128)(2,1)}, bf16[384,384]{1,0:T(8,128)(2,1)}, u32[]{:S(2)}, u32[]{:S(2)}) collective-permute-start(bf16[384,384]{1,0:T(8,128)(2,1)} %fusion.43), channel_id=1, source_target_pairs={{0,1},{1,0},{2,3},{3,2},{4,5},{5,4},{6,7},{7,6},{8,9},{9,8},{10,11... | collective-permute-start | bytes 884744 | tf_op jit(solution)/shard_map/ppermute | solution.py:34
  420.4 50.8 %collective-permute-start.59 = (f32[80,384]{1,0:T(8,128)}, f32[80,384]{1,0:T(8,128)}, u32[]{:S(2)}, u32[]{:S(2)}) collective-permute-start(f32[80,384]{1,0:T(8,128)} %get-tuple-element.373), channel_id=1, source_target_pairs={{0,1},{1,0},{2,3},{3,2},{4,5},{5,4},{6,7},{7,6},{8,9},{9,8},{10,11... | collective-permute-start | bytes 368648 | tf_op jit(solution)/shard_map/ppermute | solution.py:34
  430.1 92.9 %all-gather.7.cloned.1.call-start = ((), (), s32[]{:S(2)}) async-start(), calls=%async_computation.1 | async-start | bytes 2359296 | tf_op jit(solution)/shard_map/all_gather | solution.py:706
  430.2 36.4 %collective-permute-start.63 = (bf16[768,384]{1,0:T(8,128)(2,1)}, bf16[768,384]{1,0:T(8,128)(2,1)S(1)}, u32[]{:S(2)}, u32[]{:S(2)}) collective-permute-start(bf16[768,384]{1,0:T(8,128)(2,1)} %add_convert_fusion.2), channel_id=1, source_target_pairs={{0,16},{4,20},{8,24},{12,28},{16,0},{20,4},{24,8},{28,12},{1,17},{... | collective-permute-start | bytes 1769480 | tf_op jit(solution)/shard_map/ppermute | solution.py:39
  436.3 34.7 %collective-permute-start.52 = (f32[1024,384]{1,0:T(8,128)S(1)}, f32[1024,384]{1,0:T(8,128)S(1)}, u32[]{:S(2)}, u32[]{:S(2)}) collective-permute-start(f32[1024,384]{1,0:T(8,128)S(1)} %copy-done.117), channel_id=1, source_target_pairs={{0,2},{2,0},{1,3},{3,1},{4,6},{6,4},{5,7},{7,5},{8,10},{10,8},{9,1... | collective-permute-start | bytes 4718600 | tf_op jit(solution)/shard_map/ppermute | solution.py:34
  497.1 28.9 %collective-permute-start.74 = (bf16[192,1536]{1,0:T(8,128)(2,1)S(1)}, bf16[192,1536]{1,0:T(8,128)(2,1)}, u32[]{:S(2)}, u32[]{:S(2)}) collective-permute-start(bf16[192,1536]{1,0:T(8,128)(2,1)S(1)} %maximum_select_fusion.refs_0_), channel_id=1, source_target_pairs={{0,4},{4,0},{8,12},{12,8},{16,20},{20,16},{24,28},{28,24},{1,5},{5... | collective-permute-start | bytes 1769480 | tf_op jit(solution)/shard_map/ppermute | solution.py:39
  498.5 31.4 %collective-permute-start.73 = (bf16[192,384]{1,0:T(8,128)(2,1)}, bf16[192,384]{1,0:T(8,128)(2,1)}, u32[]{:S(2)}, u32[]{:S(2)}) collective-permute-start(bf16[192,384]{1,0:T(8,128)(2,1)} %add_convert_fusion.18.refs_2_), channel_id=1, source_target_pairs={{0,4},{4,0},{8,12},{12,8},{16,20},{20,16},{24,28},{28,24},{1,5},{5... | collective-permute-start | bytes 442376 | tf_op jit(solution)/shard_map/ppermute | solution.py:39
  499.2 30.7 %collective-permute-start.72 = (bf16[192,1152]{1,0:T(8,128)(2,1)S(1)}, bf16[192,1152]{1,0:T(8,128)(2,1)}, u32[]{:S(2)}, u32[]{:S(2)}) collective-permute-start(bf16[192,1152]{1,0:T(8,128)(2,1)S(1)} %maximum_select_fusion.1.refs_0_), channel_id=1, source_target_pairs={{0,4},{4,0},{8,12},{12,8},{16,20},{20,16},{24,28},{28,24},{1,5},{5... | collective-permute-start | bytes 1327112 | tf_op jit(solution)/shard_map/ppermute | solution.py:39
  (189 other events, 1541.2 us)
Sparse Core Ops, SparseCore 0:
  430.2 26.0 all-gather.4
  497.2 25.8 all-gather.6

commit v2 on v1

--- a/solution.py
+++ b/solution.py
@@ -999,7 +999,9 @@
         up_grad = matmul(keep.first_low, grad_inner)
         chains[layer, UP] = Reduce(line.mark(line.next(up_grad[half:]).astype(BF16)), final)
         chains[layer, UP].own = up_grad[:half]
-        chains[layer, DOWN].own = matmul(keep.active, low_own)
+        down_low = low_own
+        if final:
+            chains[layer, DOWN].own = matmul(keep.active, down_low)
         steps((above, DOWN), (above, UP))
         *grad_hidden, low_own, low_other, grad_mixed, first_sums = kernel(
             partial(first_norm_kernel, layer),
@@ -1010,6 +1012,8 @@
         )
         out_other = matmul_low(keep.mixed, low_other)
         out_own = matmul(keep.mixed, low_own)
+        if not final:
+            chains[layer, DOWN].own = matmul(keep.active, down_low)
         split_terms[2 * layer : 2 * layer + 2] = [second_sums, first_sums]
         whole_terms[2 * layer + 1] = up_sums
         steps((above, QKV, 0), (layer, DOWN))

time: 548 us -> 547 us (level)
  starting transfers between devices: 88.4 us -> 80.4 us
  waiting for transfers between devices: 85.2 us -> 91.7 us
    ppermute x39, starting transfers between devices: 56.1 us -> 48.4 us  [swap_bit(): return lax.ppermute(value, DP, [(i, i ^ 1 << bit) for i in range(count)])]
    unnamed x293 -> x287, local copies, waits for them, and re-layouts: 30.6 us -> 29.2 us
where the time goes in v2:
time: 547 us; the launch traced here: 540 us
  Pallas kernels  184 us (34%)
  waiting for transfers between devices  91.7 us (17%)
  starting transfers between devices  80.4 us (15%)
  other arithmetic  67.8 us (12%)
  local copies, waits for them, and re-layouts  62 us (11%)
  matrix products  36.8 us (7%)
  between operations  16.5 us (3%)
    pallas_call x14, Pallas kernels, token_kernel(): pl.pallas_call(kernel, grid=(length // block,), in_specs=in_specs, out_sp...  93 us
    ppermute x39, waiting for transfers between devices, swap_bit(): return lax.ppermute(value, DP, [(i, i ^ 1 << bit) for i in range(count)])  59 us
    pallas_call x3, Pallas kernels, attend_backward(): pl.pallas_call(partial(backward_kernel, scale=scale, start=start), grid_s...  51.9 us
    ppermute x39, starting transfers between devices, swap_bit(): return lax.ppermute(value, DP, [(i, i ^ 1 << bit) for i in range(count)])  48.4 us
    dot_general x16, matrix products, dot_tn(): lax.dot_general(left, right, (((0,), (0,)), ((), ())), preferred_element_...  36.8 us
    convert_element_type x26, other arithmetic, step(): self.sent = sum((part.astype(F32) for part in parts)).astype(BF16)  32.9 us
    unnamed x287, local copies, waits for them, and re-layouts  29.2 us
    ppermute x30, waiting for transfers between devices, swap(): return lax.ppermute(value, axis, [(0, 1), (1, 0)])  26.6 us
  transfers between devices with their start and end apart: 77, of which 26 were waited for; matrix products, arithmetic and copies ran while one was open for 26% of the time, Pallas kernels for 27%

profile of v2, /device:TPU:0, one launch (start us, length us, event | category | flops | bytes accessed | tf_op | source)
XLA Modules:
  0.0 539.5 jit_solution(16047919697099137520)
XLA Ops:
  33.4 4.9 collective-permute-start.5
  42.0 6.9 %collective-permute-done.4.refs_6_.refs_5_ = bf16[192,1152]{1,0:T(8,128)(2,1)S(1)} collective-permute-done((bf16[192,1152]{1,0:T(8,128)(2,1)S(1)}, bf16[192,1152]{1,0:T(8,128)(2,1)S(1)}, u32[]{:S(2)}, u32[]{:S(2)}) %collective-permute-start.4) | collective-permute-done | bytes 442400 | tf_op jit(solution)/shard_map/ppermute | solution.py:39
  69.5 12.5 %shard_map.298 = (bf16[1024,384]{1,0:T(8,128)(2,1)S(1)}, f32[3,16,128]{2,1,0:T(8,128)S(1)}) custom-call(s32[3,14,11]{2,1,0:T(8,128)S(1)} %bitcast.165, s32[3]{0:T(128)S(1)} %get-tuple-element.442.most_ref, bf16[1024,1152]{1,0:T(8,128)(2,1)S(1)} %shard_map.297.q_ref.k_ref.v_ref, bf16[1024,1152]{1,0:T(8,128)(2,1)S(1)} %shard_map.297.q_ref.k_ref.v_ref, ...), custom_call_target="tpu_custom_call" | custom-call | tf_op jit(solution)/shard_map/pallas_call | solution.py:361
  94.1 5.9 %collective-permute-done.13.refs_10_.refs_4_ = bf16[192,1152]{1,0:T(8,128)(2,1)S(1)} collective-permute-done((bf16[192,1152]{1,0:T(8,128)(2,1)S(1)}, bf16[192,1152]{1,0:T(8,128)(2,1)S(1)}, u32[]{:S(2)}, u32[]{:S(2)}) %collective-permute-start.13) | collective-permute-done | bytes 442400 | tf_op jit(solution)/shard_map/ppermute | solution.py:39
  102.6 13.7 %shard_map.300 = (bf16[1024,384]{1,0:T(8,128)(2,1)}, bf16[1024,384]{1,0:T(8,128)(2,1)}, f32[1024,768]{1,0:T(8,128)}, bf16[1024,768]{1,0:T(8,128)(2,1)}, bf16[102...) custom-call(s32[1,1]{1,0:T(1,128)} %bitcast.refs_0_.place_ref, ...), custom_call_target="tpu_custom_call" | custom-call | tf_op jit(solution)/shard_map/pallas_call | solution.py:483
  126.2 7.3 %shard_map.301 = (f32[1024,768]{1,0:T(8,128)}, bf16[1024,384]{1,0:T(8,128)(2,1)S(1)}, bf16[1024,384]{1,0:T(8,128)(2,1)S(1)}, bf16[1024,768]{1,0:T(8,128)(2,1)}, ...) custom-call(s32[1,1]{1,0:T(1,128)} %bitcast.refs_0_.place_ref, bf16[1024,384]{1,0:T(8,128)(2,1)} %get-tuple-element.246.refs_1_, ...), custom_call_target="tpu_custom_call" | custom-call | tf_op jit(solution)/shard_map/pallas_call | solution.py:483
  138.6 12.7 %shard_map.302 = (bf16[1024,384]{1,0:T(8,128)(2,1)S(1)}, f32[3,16,128]{2,1,0:T(8,128)S(1)}) custom-call(s32[3,14,11]{2,1,0:T(8,128)S(1)} %bitcast.168, s32[3]{0:T(128)S(1)} %copy-done.96, bf16[1024,1152]{1,0:T(8,128)(2,1)S(1)} %copy-done.2, bf16[1024,1152]{1,0:T(8,128)(2,1)S(1)} %copy-done.2, bf16[1024,1152]{1,0:T(8,128)(2,1)S(1)} %copy-done.2, ...), custom_call_target="tpu_custom_call" | custom-call | tf_op jit(solution)/shard_map/pallas_call | solution.py:361
  151.4 7.0 %collective-permute-done.20.refs_12_.refs_5_ = bf16[1536,384]{1,0:T(8,128)(2,1)} collective-permute-done((bf16[1536,384]{1,0:T(8,128)(2,1)}, bf16[1536,384]{1,0:T(8,128)(2,1)}, u32[]{:S(2)}, u32[]{:S(2)}) %collective-permute-start.20) | collective-permute-done | bytes 1179680 | tf_op jit(solution)/shard_map/ppermute | solution.py:34
  164.8 14.0 %shard_map.304 = (bf16[1024,384]{1,0:T(8,128)(2,1)S(1)}, bf16[1024,384]{1,0:T(8,128)(2,1)S(1)}, f32[1024,768]{1,0:T(8,128)}, bf16[1024,768]{1,0:T(8,128)(2,1)}, ...) custom-call(s32[1,1]{1,0:T(1,128)} %bitcast.refs_0_.place_ref, ...), custom_call_target="tpu_custom_call" | custom-call | tf_op jit(solution)/shard_map/pallas_call | solution.py:483
  186.7 7.3 %shard_map.305 = (f32[1024,768]{1,0:T(8,128)}, f32[1024,384]{1,0:T(8,128)}, bf16[1024,384]{1,0:T(8,128)(2,1)S(1)}, bf16[1024,384]{1,0:T(8,128)(2,1)S(1)}, bf16[1...) custom-call(s32[1,1]{1,0:T(1,128)} %bitcast.refs_0_.place_ref, ...), custom_call_target="tpu_custom_call" | custom-call | tf_op jit(solution)/shard_map/pallas_call | solution.py:483
  196.9 9.5 %shard_map.306 = (bf16[1024,768]{1,0:T(8,128)(2,1)}, bf16[1024,1536]{1,0:T(8,128)(2,1)}, f32[8,384]{1,0:T(8,128)S(1)}) custom-call(s32[1,1]{1,0:T(1,128)} %bitcast.refs_0_.place_ref, bf16[1024,384]{1,0:T(8,128)(2,1)S(1)} %get-tuple-element.289.refs_1_, bf16[1024,384]{1,0:T(8,128)(2,1)S(1)} %get-tuple-element.272.refs_2_, ...), custom_call_target="tpu_custom_call" | custom-call | tf_op jit(solution)/shard_map/pallas_call | solution.py:483
  208.2 5.0 fusion.30
  215.6 6.4 %shard_map.307 = (f32[1024,384]{1,0:T(8,128)S(1)}, f32[1024,384]{1,0:T(8,128)}, bf16[1024,384]{1,0:T(8,128)(2,1)S(1)}, bf16[1024,384]{1,0:T(8,128)(2,1)S(1)}, bf...) custom-call(s32[1,1]{1,0:T(1,128)} %bitcast.refs_0_.place_ref, bf16[1024,768]{1,0:T(8,128)(2,1)} %get-tuple-element.280.refs_1_, ...), custom_call_target="tpu_custom_call" | custom-call | tf_op jit(solution)/shard_map/pallas_call | solution.py:483
  226.8 9.2 %collective-permute-done.30 = bf16[1536,384]{1,0:T(8,128)(2,1)} collective-permute-done((bf16[1536,384]{1,0:T(8,128)(2,1)}, bf16[1536,384]{1,0:T(8,128)(2,1)}, u32[]{:S(2)}, u32[]{:S(2)}) %collective-permute-start.30) | collective-permute-done | bytes 1179680 | tf_op jit(solution)/shard_map/ppermute | solution.py:34
  238.9 25.8 %shard_map.308.refs_1_ = bf16[1024,1152]{1,0:T(8,128)(2,1)S(1)} custom-call(s32[3,14,11]{2,1,0:T(8,128)S(1)} %bitcast.169, s32[3]{0:T(128)S(1)} %copy-done.97, bf16[1024,1152]{1,0:T(8,128)(2,1)} %get-tuple-element.251.q_ref.k_ref.v_ref, bf16[1024,1152]{1,0:T(8,128)(2,1)} %get-tuple-element.251.q_ref.k_ref.v_ref, ...), custom_call_target="tpu_custom_call" | custom-call | tf_op jit(solution)/shard_map/pallas_call | solution.py:387
  271.3 3.9 shard_map.309
  286.3 5.7 %shard_map.310 = (f32[1024,768]{1,0:T(8,128)}, bf16[1024,384]{1,0:T(8,128)(2,1)S(1)}, bf16[1024,384]{1,0:T(8,128)(2,1)S(1)}, f32[8,768]{1,0:T(8,128)S(1)}) custom-call(s32[1,1]{1,0:T(1,128)} %bitcast.refs_0_.place_ref, bf16[1024,768]{1,0:T(8,128)(2,1)} %get-tuple-element.301.refs_1_, bf16[1024,768]{1,0:T(8,128)(2,1)} %collective-permute-done.33.refs_2_, ...), custom_call_target="tpu_custom_call" | custom-call | tf_op jit(solution)/shard_map/pallas_call | solution.py:483
  292.1 4.9 fusion.36
  308.0 9.1 %shard_map.311 = (bf16[1024,768]{1,0:T(8,128)(2,1)S(1)}, bf16[1024,1536]{1,0:T(8,128)(2,1)}, f32[8,384]{1,0:T(8,128)S(1)}) custom-call(s32[1,1]{1,0:T(1,128)} %bitcast.refs_0_.place_ref, bf16[1024,384]{1,0:T(8,128)(2,1)S(1)} %get-tuple-element.320.refs_1_, bf16[1024,384]{1,0:T(8,128)(2,1)S(1)} %get-tuple-element.309.refs_2_, ...), custom_call_target="tpu_custom_call" | custom-call | tf_op jit(solution)/shard_map/pallas_call | solution.py:483
  317.2 5.1 fusion.37
  337.7 6.4 %shard_map.312 = (f32[1024,384]{1,0:T(8,128)S(1)}, f32[1024,384]{1,0:T(8,128)}, bf16[1024,384]{1,0:T(8,128)(2,1)S(1)}, bf16[1024,384]{1,0:T(8,128)(2,1)S(1)}, bf...) custom-call(s32[1,1]{1,0:T(1,128)} %bitcast.refs_0_.place_ref, bf16[1024,768]{1,0:T(8,128)(2,1)} %copy-done.40, ...), custom_call_target="tpu_custom_call" | custom-call | tf_op jit(solution)/shard_map/pallas_call | solution.py:483
  352.9 17.4 %shard_map.313.refs_1_ = bf16[1024,768]{1,0:T(8,128)(2,1)S(1)} custom-call(s32[3,14,11]{2,1,0:T(8,128)S(1)} %bitcast.166, s32[3]{0:T(128)S(1)} %get-tuple-element.442.most_ref, bf16[1024,1152]{1,0:T(8,128)(2,1)S(1)} %shard_map.297.q_ref.k_ref.v_ref, bf16[1024,1152]{1,0:T(8,128)(2,1)S(1)} %shard_map.297.q_ref.k_ref.v_ref, ...), custom_call_target="tpu_custom_call" | custom-call | tf_op jit(solution)/shard_map/pallas_call | solution.py:387
  392.0 8.8 %shard_map.314.refs_2_ = bf16[1024,384]{1,0:T(8,128)(2,1)S(1)} custom-call(s32[3,14,11]{2,1,0:T(8,128)S(1)} %bitcast.167, s32[3]{0:T(128)S(1)} %get-tuple-element.442.most_ref, bf16[1024,1152]{1,0:T(8,128)(2,1)S(1)} %shard_map.297.q_ref.k_ref.v_ref, bf16[1024,1152]{1,0:T(8,128)(2,1)S(1)} %shard_map.297.q_ref.k_ref.v_ref, ...), custom_call_target="tpu_custom_call" | custom-call | tf_op jit(solution)/shard_map/pallas_call | solution.py:387
  439.0 11.8 %collective-permute-done.58 = bf16[96,1152]{1,0:T(8,128)(2,1)S(1)} collective-permute-done((bf16[96,1152]{1,0:T(8,128)(2,1)S(1)}, bf16[96,1152]{1,0:T(8,128)(2,1)S(1)}, u32[]{:S(2)}, u32[]{:S(2)}) %collective-permute-start.58) | collective-permute-done | bytes 221216 | tf_op jit(solution)/shard_map/ppermute | solution.py:39
  455.1 10.0 %collective-permute-done.63 = bf16[768,384]{1,0:T(8,128)(2,1)S(1)} collective-permute-done((bf16[768,384]{1,0:T(8,128)(2,1)}, bf16[768,384]{1,0:T(8,128)(2,1)S(1)}, u32[]{:S(2)}, u32[]{:S(2)}) %collective-permute-start.63) | collective-permute-done | bytes 589856 | tf_op jit(solution)/shard_map/ppermute | solution.py:39
  473.9 5.2 collective-permute-done.65.refs_1_
  484.3 4.6 collective-permute-done.70
  489.7 3.9 collective-permute-done.68
  498.5 4.6 collective-permute-done.71
  513.0 3.6 fusion
  524.3 3.9 shard_map.319
  528.2 4.3 shard_map.320
  (580 shorter events, 261.8 us)
Async XLA Ops:
  7.2 505.8 %all-gather.5.cloned.1.call-start = ((), (), s32[]{:S(2)}) async-start(), calls=%async_computation | async-start | bytes 2359296 | tf_op jit(solution)/shard_map/all_gather | solution.py:706
  39.8 21.9 %collective-permute-start.6 = (bf16[192,1536]{1,0:T(8,128)(2,1)}, bf16[192,1536]{1,0:T(8,128)(2,1)}, u32[]{:S(2)}, u32[]{:S(2)}) collective-permute-start(bf16[192,1536]{1,0:T(8,128)(2,1)} %dynamic-slice_bitcast_fusion.1), channel_id=1, source_target_pairs={{0,1},{1,0},{2,3},{3,2},{4,5},{5,4},{6,7},{7,6},{8,9},{9,8},{10,11... | collective-permute-start | bytes 1769480 | tf_op jit(solution)/shard_map/ppermute | solution.py:34
  61.8 20.8 %collective-permute-start.10 = (bf16[192,1536]{1,0:T(8,128)(2,1)}, bf16[192,1536]{1,0:T(8,128)(2,1)}, u32[]{:S(2)}, u32[]{:S(2)}) collective-permute-start(bf16[192,1536]{1,0:T(8,128)(2,1)} %collective-permute-done.6.refs_10_.refs_8_), channel_id=1, source_target_pairs={{0,4},{4,0},{8,12},{12,8},{16,20},{20,16},{24,28},{28,24},{1,5},{5... | collective-permute-start | bytes 1769480 | tf_op jit(solution)/shard_map/ppermute | solution.py:39
  65.0 21.1 %collective-permute-start.16 = (f32[6,2,384]{2,0,1:T(8,128)}, f32[6,2,384]{2,0,1:T(8,128)}, u32[]{:S(2)}, u32[]{:S(2)}) collective-permute-start(f32[6,2,384]{2,0,1:T(8,128)} %stack.34), channel_id=1, source_target_pairs={{0,1},{1,0},{2,3},{3,2},{4,5},{5,4},{6,7},{7,6},{8,9},{9,8},{10,11... | collective-permute-start | bytes 55304 | tf_op jit(solution)/shard_map/ppermute | solution.py:34
  119.3 39.1 %collective-permute-start.20 = (bf16[1536,384]{1,0:T(8,128)(2,1)}, bf16[1536,384]{1,0:T(8,128)(2,1)}, u32[]{:S(2)}, u32[]{:S(2)}) collective-permute-start(bf16[1536,384]{1,0:T(8,128)(2,1)} %slice_bitcast_fusion), channel_id=1, source_target_pairs={{0,1},{1,0},{2,3},{3,2},{4,5},{5,4},{6,7},{7,6},{8,9},{9,8},{10,11... | collective-permute-start | bytes 3538952 | tf_op jit(solution)/shard_map/ppermute | solution.py:34
  206.8 29.1 %collective-permute-start.30 = (bf16[1536,384]{1,0:T(8,128)(2,1)}, bf16[1536,384]{1,0:T(8,128)(2,1)}, u32[]{:S(2)}, u32[]{:S(2)}) collective-permute-start(bf16[1536,384]{1,0:T(8,128)(2,1)} %fusion.29), channel_id=1, source_target_pairs={{0,1},{1,0},{2,3},{3,2},{4,5},{5,4},{6,7},{7,6},{8,9},{9,8},{10,11... | collective-permute-start | bytes 3538952 | tf_op jit(solution)/shard_map/ppermute | solution.py:34
  214.4 54.7 %collective-permute-start.31 = (bf16[384,1536]{1,0:T(8,128)(2,1)}, bf16[384,1536]{1,0:T(8,128)(2,1)}, u32[]{:S(2)}, u32[]{:S(2)}) collective-permute-start(bf16[384,1536]{1,0:T(8,128)(2,1)} %slice.125), channel_id=1, source_target_pairs={{0,1},{1,0},{2,3},{3,2},{4,5},{5,4},{6,7},{7,6},{8,9},{9,8},{10,11... | collective-permute-start | bytes 3538952 | tf_op jit(solution)/shard_map/ppermute | solution.py:34
  237.2 29.8 %collective-permute-start.32 = (bf16[768,384]{1,0:T(8,128)(2,1)S(1)}, bf16[768,384]{1,0:T(8,128)(2,1)S(1)}, u32[]{:S(2)}, u32[]{:S(2)}) collective-permute-start(bf16[768,384]{1,0:T(8,128)(2,1)S(1)} %fusion.7), channel_id=1, source_target_pairs={{0,4},{4,0},{8,12},{12,8},{16,20},{20,16},{24,28},{28,24},{1,5},{5... | collective-permute-start | bytes 1769480 | tf_op jit(solution)/shard_map/ppermute | solution.py:39
  276.5 29.1 %collective-permute-start.34 = (bf16[384,1536]{1,0:T(8,128)(2,1)}, bf16[384,1536]{1,0:T(8,128)(2,1)}, u32[]{:S(2)}, u32[]{:S(2)}) collective-permute-start(bf16[384,1536]{1,0:T(8,128)(2,1)} %pad_maximum_fusion.2), channel_id=1, source_target_pairs={{0,1},{1,0},{2,3},{3,2},{4,5},{5,4},{6,7},{7,6},{8,9},{9,8},{10,11... | collective-permute-start | bytes 3538952 | tf_op jit(solution)/shard_map/ppermute | solution.py:34
  297.0 53.3 %collective-permute-start.40 = (bf16[1536,384]{1,0:T(8,128)(2,1)}, bf16[1536,384]{1,0:T(8,128)(2,1)}, u32[]{:S(2)}, u32[]{:S(2)}) collective-permute-start(bf16[1536,384]{1,0:T(8,128)(2,1)} %fusion.36), channel_id=1, source_target_pairs={{0,1},{1,0},{2,3},{3,2},{4,5},{5,4},{6,7},{7,6},{8,9},{9,8},{10,11... | collective-permute-start | bytes 3538952 | tf_op jit(solution)/shard_map/ppermute | solution.py:34
  297.9 31.6 %collective-permute-start.38 = (bf16[768,384]{1,0:T(8,128)(2,1)S(1)}, bf16[768,384]{1,0:T(8,128)(2,1)}, u32[]{:S(2)}, u32[]{:S(2)}) collective-permute-start(bf16[768,384]{1,0:T(8,128)(2,1)S(1)} %add_convert_fusion.10), channel_id=1, source_target_pairs={{0,16},{4,20},{8,24},{12,28},{16,0},{20,4},{24,8},{28,12},{1,17},{... | collective-permute-start | bytes 1769480 | tf_op jit(solution)/shard_map/ppermute | solution.py:39
  301.8 30.2 %collective-permute-start.37 = (bf16[192,1536]{1,0:T(8,128)(2,1)S(1)}, bf16[192,1536]{1,0:T(8,128)(2,1)}, u32[]{:S(2)}, u32[]{:S(2)}) collective-permute-start(bf16[192,1536]{1,0:T(8,128)(2,1)S(1)} %fusion.3), channel_id=1, source_target_pairs={{0,8},{4,12},{8,0},{12,4},{16,24},{20,28},{24,16},{28,20},{1,9},{5... | collective-permute-start | bytes 1769480 | tf_op jit(solution)/shard_map/ppermute | solution.py:39
  307.6 38.6 %collective-permute-start.41 = (bf16[192,1536]{1,0:T(8,128)(2,1)}, bf16[192,1536]{1,0:T(8,128)(2,1)}, u32[]{:S(2)}, u32[]{:S(2)}) collective-permute-start(bf16[192,1536]{1,0:T(8,128)(2,1)} %fusion.9), channel_id=1, source_target_pairs={{0,4},{4,0},{8,12},{12,8},{16,20},{20,16},{24,28},{28,24},{1,5},{5... | collective-permute-start | bytes 1769480 | tf_op jit(solution)/shard_map/ppermute | solution.py:39
  329.5 58.4 %collective-permute-start.42 = (bf16[384,1536]{1,0:T(8,128)(2,1)}, bf16[384,1536]{1,0:T(8,128)(2,1)}, u32[]{:S(2)}, u32[]{:S(2)}) collective-permute-start(bf16[384,1536]{1,0:T(8,128)(2,1)} %slice.127), channel_id=1, source_target_pairs={{0,1},{1,0},{2,3},{3,2},{4,5},{5,4},{6,7},{7,6},{8,9},{9,8},{10,11... | collective-permute-start | bytes 3538952 | tf_op jit(solution)/shard_map/ppermute | solution.py:34
  332.1 42.3 %collective-permute-start.46 = (bf16[768,384]{1,0:T(8,128)(2,1)S(1)}, bf16[768,384]{1,0:T(8,128)(2,1)S(1)}, u32[]{:S(2)}, u32[]{:S(2)}) collective-permute-start(bf16[768,384]{1,0:T(8,128)(2,1)S(1)} %add_convert_fusion.8.refs_2_), channel_id=1, source_target_pairs={{0,4},{4,0},{8,12},{12,8},{16,20},{20,16},{24,28},{28,24},{1,5},{5... | collective-permute-start | bytes 1769480 | tf_op jit(solution)/shard_map/ppermute | solution.py:39
  335.0 40.9 %collective-permute-start.45 = (bf16[192,1536]{1,0:T(8,128)(2,1)S(1)}, bf16[192,1536]{1,0:T(8,128)(2,1)S(1)}, u32[]{:S(2)}, u32[]{:S(2)}) collective-permute-start(bf16[192,1536]{1,0:T(8,128)(2,1)S(1)} %add_convert_fusion.7), channel_id=1, source_target_pairs={{0,16},{4,20},{8,24},{12,28},{16,0},{20,4},{24,8},{28,12},{1,17},{... | collective-permute-start | bytes 1769480 | tf_op jit(solution)/shard_map/ppermute | solution.py:39
  348.7 33.9 %collective-permute-start.44 = (bf16[192,1536]{1,0:T(8,128)(2,1)}, bf16[192,1536]{1,0:T(8,128)(2,1)}, u32[]{:S(2)}, u32[]{:S(2)}) collective-permute-start(bf16[192,1536]{1,0:T(8,128)(2,1)} %fusion.2), channel_id=1, source_target_pairs={{0,8},{4,12},{8,0},{12,4},{16,24},{20,28},{24,16},{28,20},{1,9},{5... | collective-permute-start | bytes 1769480 | tf_op jit(solution)/shard_map/ppermute | solution.py:39
  352.3 32.5 %collective-permute-start.43 = (bf16[768,384]{1,0:T(8,128)(2,1)}, bf16[768,384]{1,0:T(8,128)(2,1)}, u32[]{:S(2)}, u32[]{:S(2)}) collective-permute-start(bf16[768,384]{1,0:T(8,128)(2,1)} %fusion.10), channel_id=1, source_target_pairs={{0,4},{4,0},{8,12},{12,8},{16,20},{20,16},{24,28},{28,24},{1,5},{5... | collective-permute-start | bytes 1769480 | tf_op jit(solution)/shard_map/ppermute | solution.py:39
  375.2 38.8 %collective-permute-start.50 = (bf16[384,1152]{1,0:T(8,128)(2,1)}, bf16[384,1152]{1,0:T(8,128)(2,1)}, u32[]{:S(2)}, u32[]{:S(2)}) collective-permute-start(bf16[384,1152]{1,0:T(8,128)(2,1)} %pad_maximum_fusion.3), channel_id=1, source_target_pairs={{0,1},{1,0},{2,3},{3,2},{4,5},{5,4},{6,7},{7,6},{8,9},{9,8},{10,11... | collective-permute-start | bytes 2654216 | tf_op jit(solution)/shard_map/ppermute | solution.py:34
  378.2 31.4 %collective-permute-start.51 = (bf16[192,1536]{1,0:T(8,128)(2,1)S(1)}, bf16[192,1536]{1,0:T(8,128)(2,1)S(1)}, u32[]{:S(2)}, u32[]{:S(2)}) collective-permute-start(bf16[192,1536]{1,0:T(8,128)(2,1)S(1)} %add_convert_fusion.5.refs_2_), channel_id=1, source_target_pairs={{0,4},{4,0},{8,12},{12,8},{16,20},{20,16},{24,28},{28,24},{1,5},{5... | collective-permute-start | bytes 1769480 | tf_op jit(solution)/shard_map/ppermute | solution.py:39
  387.4 31.4 %collective-permute-start.49 = (bf16[768,384]{1,0:T(8,128)(2,1)}, bf16[768,384]{1,0:T(8,128)(2,1)}, u32[]{:S(2)}, u32[]{:S(2)}) collective-permute-start(bf16[768,384]{1,0:T(8,128)(2,1)} %fusion.1), channel_id=1, source_target_pairs={{0,8},{4,12},{8,0},{12,4},{16,24},{20,28},{24,16},{28,20},{1,9},{5... | collective-permute-start | bytes 1769480 | tf_op jit(solution)/shard_map/ppermute | solution.py:39
  390.5 31.3 %collective-permute-start.48 = (bf16[192,1536]{1,0:T(8,128)(2,1)}, bf16[192,1536]{1,0:T(8,128)(2,1)}, u32[]{:S(2)}, u32[]{:S(2)}) collective-permute-start(bf16[192,1536]{1,0:T(8,128)(2,1)} %get-tuple-element.421), channel_id=1, source_target_pairs={{0,4},{4,0},{8,12},{12,8},{16,20},{20,16},{24,28},{28,24},{1,5},{5... | collective-permute-start | bytes 1769480 | tf_op jit(solution)/shard_map/ppermute | solution.py:39
  390.9 37.9 %collective-permute-start.53 = (bf16[192,1536]{1,0:T(8,128)(2,1)}, bf16[192,1536]{1,0:T(8,128)(2,1)}, u32[]{:S(2)}, u32[]{:S(2)}) collective-permute-start(bf16[192,1536]{1,0:T(8,128)(2,1)} %add_convert_fusion.4), channel_id=1, source_target_pairs={{0,16},{4,20},{8,24},{12,28},{16,0},{20,4},{24,8},{28,12},{1,17},{... | collective-permute-start | bytes 1769480 | tf_op jit(solution)/shard_map/ppermute | solution.py:39
  410.5 21.6 %collective-permute-start.55 = (bf16[384,384]{1,0:T(8,128)(2,1)}, bf16[384,384]{1,0:T(8,128)(2,1)}, u32[]{:S(2)}, u32[]{:S(2)}) collective-permute-start(bf16[384,384]{1,0:T(8,128)(2,1)} %fusion.43), channel_id=1, source_target_pairs={{0,1},{1,0},{2,3},{3,2},{4,5},{5,4},{6,7},{7,6},{8,9},{9,8},{10,11... | collective-permute-start | bytes 884744 | tf_op jit(solution)/shard_map/ppermute | solution.py:34
  418.8 51.1 %collective-permute-start.59 = (f32[80,384]{1,0:T(8,128)}, f32[80,384]{1,0:T(8,128)}, u32[]{:S(2)}, u32[]{:S(2)}) collective-permute-start(f32[80,384]{1,0:T(8,128)} %get-tuple-element.373), channel_id=1, source_target_pairs={{0,1},{1,0},{2,3},{3,2},{4,5},{5,4},{6,7},{7,6},{8,9},{9,8},{10,11... | collective-permute-start | bytes 368648 | tf_op jit(solution)/shard_map/ppermute | solution.py:34
  428.7 92.6 %all-gather.7.cloned.1.call-start = ((), (), s32[]{:S(2)}) async-start(), calls=%async_computation.1 | async-start | bytes 2359296 | tf_op jit(solution)/shard_map/all_gather | solution.py:706
  428.8 36.4 %collective-permute-start.63 = (bf16[768,384]{1,0:T(8,128)(2,1)}, bf16[768,384]{1,0:T(8,128)(2,1)S(1)}, u32[]{:S(2)}, u32[]{:S(2)}) collective-permute-start(bf16[768,384]{1,0:T(8,128)(2,1)} %add_convert_fusion.2), channel_id=1, source_target_pairs={{0,16},{4,20},{8,24},{12,28},{16,0},{20,4},{24,8},{28,12},{1,17},{... | collective-permute-start | bytes 1769480 | tf_op jit(solution)/shard_map/ppermute | solution.py:39
  434.4 35.1 %collective-permute-start.52 = (f32[1024,384]{1,0:T(8,128)S(1)}, f32[1024,384]{1,0:T(8,128)S(1)}, u32[]{:S(2)}, u32[]{:S(2)}) collective-permute-start(f32[1024,384]{1,0:T(8,128)S(1)} %copy-done.117), channel_id=1, source_target_pairs={{0,2},{2,0},{1,3},{3,1},{4,6},{6,4},{5,7},{7,5},{8,10},{10,8},{9,1... | collective-permute-start | bytes 4718600 | tf_op jit(solution)/shard_map/ppermute | solution.py:34
  452.4 21.3 %collective-permute-start.66 = (bf16[96,1536]{1,0:T(8,128)(2,1)S(1)}, bf16[96,1536]{1,0:T(8,128)(2,1)S(1)}, u32[]{:S(2)}, u32[]{:S(2)}) collective-permute-start(bf16[96,1536]{1,0:T(8,128)(2,1)S(1)} %fusion.12), channel_id=1, source_target_pairs={{0,16},{4,20},{8,24},{12,28},{16,0},{20,4},{24,8},{28,12},{1,17},{... | collective-permute-start | bytes 884744 | tf_op jit(solution)/shard_map/ppermute | solution.py:39
  495.7 28.5 %collective-permute-start.74 = (bf16[192,1536]{1,0:T(8,128)(2,1)S(1)}, bf16[192,1536]{1,0:T(8,128)(2,1)}, u32[]{:S(2)}, u32[]{:S(2)}) collective-permute-start(bf16[192,1536]{1,0:T(8,128)(2,1)S(1)} %maximum_select_fusion.refs_0_), channel_id=1, source_target_pairs={{0,4},{4,0},{8,12},{12,8},{16,20},{20,16},{24,28},{28,24},{1,5},{5... | collective-permute-start | bytes 1769480 | tf_op jit(solution)/shard_map/ppermute | solution.py:39
  496.5 31.7 %collective-permute-start.73 = (bf16[192,384]{1,0:T(8,128)(2,1)}, bf16[192,384]{1,0:T(8,128)(2,1)}, u32[]{:S(2)}, u32[]{:S(2)}) collective-permute-start(bf16[192,384]{1,0:T(8,128)(2,1)} %add_convert_fusion.18.refs_2_), channel_id=1, source_target_pairs={{0,4},{4,0},{8,12},{12,8},{16,20},{20,16},{24,28},{28,24},{1,5},{5... | collective-permute-start | bytes 442376 | tf_op jit(solution)/shard_map/ppermute | solution.py:39
  497.8 30.4 %collective-permute-start.72 = (bf16[192,1152]{1,0:T(8,128)(2,1)S(1)}, bf16[192,1152]{1,0:T(8,128)(2,1)}, u32[]{:S(2)}, u32[]{:S(2)}) collective-permute-start(bf16[192,1152]{1,0:T(8,128)(2,1)S(1)} %maximum_select_fusion.1.refs_0_), channel_id=1, source_target_pairs={{0,4},{4,0},{8,12},{12,8},{16,20},{20,16},{24,28},{28,24},{1,5},{5... | collective-permute-start | bytes 1327112 | tf_op jit(solution)/shard_map/ppermute | solution.py:39
  (186 other events, 1513.2 us)
Sparse Core Ops, SparseCore 0:
  428.8 25.6 all-gather.4
  495.7 25.4 all-gather.6
